TPU v7x, 32 devices: a whole 2x2x4 slice. The times are simulated.
32 devices in a mesh: span: 8 (over y, x, core), freq: 4 (over z).
Axes of the slice: x: 2, y: 2, z: 4, core: 2. Of those that a mesh axis runs over, the one named last changes fastest.
Arguments:
- visibilities: bfloat16 [4, 256, 2, 512], P('freq', 'span'), may hold values from -6 to 6
- coords: float32 [4, 256, 2, 512], P('freq', 'span'), may hold values from -12 to 12
- vis_counts: int32 [4, 256], P('freq', 'span'), may hold values from 128 to 512
- cover_tile: int32 [4, 256, 1], P('freq', 'span'), may hold values from 0 to 7; in each aligned block of 32 rows (0 to 31, 32 to 63, ..., all dimensions but the last counted through in order) at most 8 rows name the same one
- offsets: int32 [4, 256, 2], P('freq', 'span'), may hold values from 0 to 96
- channel: int32 [4, 256], P('freq', 'span'), may hold values from 0 to 15
- taper: float32 [32, 32], replicated, may hold values from 0.2 to 1
Outputs:
- uv_terms: float32 [2, 8, 2, 128, 128], P(None, 'span')
Inputs may be any that keep to these rules, and one draw needn't show every extreme that they name: `cover_tile`: the subgrids of one device name each tile at most 8 times, a bound that some block reaches.
All inputs are finite; a program needn't handle non-finite values.
Results may differ from a plain program's by a relative error of at most 0.005.
Values may be sent and summed in bfloat16 or wider, within the bound.
A program may use at most 64 MiB of HBM per device.

v0:
```python
import functools
import math

import jax
import jax.numpy as jnp
import ml_dtypes
import numpy as np
from jax import lax
from jax.experimental import pallas as pl
from jax.experimental.pallas import tpu as pltpu
from jax.sharding import PartitionSpec as P

TILE = 128
NT = 2
CH_DEV = 16
SUB = 32
MESH = pl.DeviceIdType.MESH
F32 = jnp.float32
BF16 = jnp.bfloat16


def dft_constants():
    centred = np.arange(32) - 16.0
    angle = -2.0 * np.pi * centred[:, None] * centred[None, :] / 32.0
    f_re, f_im = np.cos(angle), np.sin(angle)
    right = np.block([[f_re.T, f_im.T], [-f_im.T, f_re.T]])
    right_i = np.block([[-f_im.T, f_re.T], [-f_re.T, -f_im.T]])
    both = np.concatenate([right, right_i], 1)
    left = np.block([[f_re, -f_im], [f_im, f_re]]) / 32.0
    rows, cols = np.arange(128), np.arange(512)
    repeat = (rows[:, None] // 32 == cols[None, :] // 128) & (
        rows[:, None] % 32 == cols[None, :] % 32
    )
    return [m.astype(ml_dtypes.bfloat16) for m in (both, left, repeat)]


def iota(shape, axis):
    return lax.broadcasted_iota(jnp.int32, shape, axis)


def unit_phase(turns):
    frac = turns - jnp.round(turns)
    half = frac * math.pi
    sq = half * half
    sin_h = sum_poly(sq, [(-1.0) ** n / math.factorial(2 * n + 1) for n in range(7)]) * half
    cos_h = sum_poly(sq, [(-1.0) ** n / math.factorial(2 * n) for n in range(8)])
    return 1.0 - 2.0 * sin_h * sin_h, 2.0 * sin_h * cos_h


def sum_poly(x, coefs):
    total = jnp.full_like(x, coefs[-1])
    for coef in coefs[-2::-1]:
        total = total * x + coef
    return total


def cmul(a, b):
    return a[0] * b[0] - a[1] * b[1], a[0] * b[1] + a[1] * b[0]


def kernel(
    n_span, n_freq, cap, rows_per, meta_ref, coord_ref, vis_ref, taper_ref, right_ref, left_ref,
    repeat_ref, out_ref, ea, eb, g_scr, y_scr, z_scr, src_v, src_s, send, got, acc_scr, rs_send,
    rs_got, ag_send, ag_got, src_sem, a_send, a_recv, r_send, r_recv, g_send, g_recv,
):
    me_s, me_f = lax.axis_index("span"), lax.axis_index("freq")
    barrier = pltpu.get_barrier_semaphore()
    for o in range(1, n_span):
        pl.semaphore_signal(
            barrier, inc=1, device_id=(lax.rem(me_s + o, n_span), me_f), device_id_type=MESH
        )
    for o in range(1, n_freq):
        pl.semaphore_signal(
            barrier, inc=1, device_id=(me_s, lax.rem(me_f + o, n_freq)), device_id_type=MESH
        )

    kk = coord_ref.shape[1] // 2
    lanes = cap * 32
    data_rows = cap * 16
    slots = n_span * cap

    meta = meta_ref[...].astype(F32)
    eye = iota((SUB, SUB), 0) == iota((SUB, SUB), 1)

    def to_rows(row):
        return jnp.sum(
            jnp.where(eye, jnp.broadcast_to(row, (SUB, SUB)), 0.0), axis=1, keepdims=True
        )

    dest_l = meta[3:4, :]
    dest_s = to_rows(dest_l)
    same = jnp.broadcast_to(dest_l, (SUB, SUB)) == dest_s
    lower = iota((SUB, SUB), 1) < iota((SUB, SUB), 0)
    upper = iota((SUB, SUB), 0) < iota((SUB, SUB), 1)
    rank_s = jnp.sum(jnp.where(same & lower, 1.0, 0.0), axis=1, keepdims=True)
    rank_l = jnp.sum(jnp.where(same & upper, 1.0, 0.0), axis=0, keepdims=True)
    slot_s = (dest_s * cap + rank_s).astype(jnp.int32)
    slot_l = (dest_l * cap + rank_l).astype(jnp.int32)
    hot = jnp.broadcast_to(slot_s, (SUB, 128)) == iota((SUB, 128), 1)
    src = jnp.sum(jnp.where(hot, iota((SUB, 128), 0).astype(F32), 0.0), axis=0, keepdims=True)
    src_v[...] = jnp.broadcast_to(src, (8, 128)).astype(jnp.int32)
    src_copy = pltpu.make_async_copy(src_v, src_s, src_sem)
    src_copy.start()
    col_s = to_rows(meta[7:8, :])
    count_s = to_rows(meta[8:9, :])
    hot_t = jnp.broadcast_to(slot_l, (slots, SUB)) == iota((slots, SUB), 0)
    col_splat = jnp.dot(
        jnp.where(hot_t, 1.0, 0.0).astype(BF16),
        jnp.broadcast_to(col_s, (SUB, 128)).astype(BF16),
        preferred_element_type=F32,
    )
    hot_x = jnp.broadcast_to(slot_s, (SUB, slots * 32)) == iota((SUB, slots * 32), 1) // 32
    spread_meta = jnp.dot(
        meta.astype(BF16), jnp.where(hot_x, 1.0, 0.0).astype(BF16), preferred_element_type=F32
    )
    eight = iota((8, 128), 0)
    for d in range(n_span):
        cols = col_splat[d * cap:(d + 1) * cap]
        if cap < 8:
            cols = jnp.concatenate([cols, jnp.zeros((8 - cap, 128), F32)], 0)
        info = spread_meta[0:8, d * lanes:d * lanes + 128]
        if lanes > 128:
            info = jnp.where(eight < 4, info, spread_meta[0:8, d * lanes + 128:d * lanes + 256])
        send[d, data_rows:, :] = jnp.concatenate([cols, info], 0).astype(BF16)

    def powers(turns):
        e1 = unit_phase(turns)
        e2 = cmul(e1, e1)
        e3 = cmul(e2, e1)
        e4 = cmul(e2, e2)
        e8 = cmul(e4, e4)
        e16 = cmul(e8, e8)
        return e1, e2, e3, e4, e8, e16

    def phases(i, carry):
        rows = pl.ds(pl.multiple_of(i * 8, 8), 8)
        for n, val in enumerate(powers(coord_ref[rows, 0:kk] * (-1.0 / 32.0))):
            ea[2 * n, rows, :] = val[0]
            ea[2 * n + 1, rows, :] = val[1]
        return carry

    lax.fori_loop(0, SUB // 8, phases, 0)
    e1, e2, e3, e4, e8, e16 = powers((coord_ref[:, kk:] - col_s) * (-1.0 / 32.0))
    live = jnp.where(
        iota((SUB, kk), 1).astype(F32) < jnp.broadcast_to(count_s, (SUB, kk)),
        1.0 / math.sqrt(kk), 0.0,
    )
    vis = vis_ref[...].astype(F32)
    w0 = (vis[:, :kk] * live, vis[:, kk:] * live)
    for n, val in enumerate([w0, cmul(w0, e1), cmul(w0, e2), cmul(w0, e3), e4, e8, e16]):
        eb[2 * n] = val[0]
        eb[2 * n + 1] = val[1]

    sub8 = iota((8, kk), 0)
    bit0, bit1, bit2 = lax.rem(sub8, 2) == 1, lax.rem(sub8 // 2, 2) == 1, sub8 >= 4
    taper = taper_ref[...]
    taper = jnp.concatenate([taper, taper], 1)
    taper = jnp.concatenate([taper, taper], 0)

    def expand(rows4, e4, e8, e16):
        low = [
            jnp.where(
                bit1, jnp.where(bit0, rows4[3][c], rows4[2][c]),
                jnp.where(bit0, rows4[1][c], rows4[0][c]),
            )
            for c in range(2)
        ]
        base = cmul(low, (jnp.where(bit2, e4[0], 1.0), jnp.where(bit2, e4[1], 0.0)))
        rr, ii = base[0] * e8[0], base[1] * e8[1]
        ri, ir = base[0] * e8[1], base[1] * e8[0]
        first = (base[0] * e16[0] + base[1] * e16[1], base[1] * e16[0] - base[0] * e16[1])
        blocks = [first, (rr + ii, ir - ri), base, (rr - ii, ri + ir)]
        return jnp.concatenate(
            [b[0] for b in blocks] + [b[1] for b in blocks], 0
        ).astype(BF16)

    def one_sub(s, carry):
        def row(ref, n):
            return tuple(
                jnp.broadcast_to(ref[2 * n + c, pl.ds(s, 1), :], (8, kk)) for c in range(2)
            )

        one = (jnp.ones((8, kk), F32), jnp.zeros((8, kk), F32))
        a_cat = expand([one] + [row(ea, n) for n in range(3)], *[row(ea, n) for n in range(3, 6)])
        b_cat = expand([row(eb, n) for n in range(4)], *[row(eb, n) for n in range(4, 7)])
        grid = lax.dot_general(
            a_cat, b_cat, (((1,), (1,)), ((), ())), preferred_element_type=F32
        )
        g_scr[pl.ds(pl.multiple_of(s * 64, 64), 64), :] = (grid * taper).astype(BF16)
        return carry

    lax.fori_loop(0, SUB, one_sub, 0, unroll=4)

    y_scr[...] = jnp.dot(
        g_scr[...], right_ref[...], preferred_element_type=F32
    ).astype(BF16)
    left = left_ref[...]

    def second(s, carry):
        part = jnp.dot(
            left, y_scr[pl.ds(pl.multiple_of(s * 64, 64), 64), :], preferred_element_type=F32
        )
        z_scr[s] = part[:32] + pltpu.roll(part[32:], 64, 1)
        return carry

    lax.fori_loop(0, SUB, second, 0, unroll=8)

    src_copy.wait()
    low_half = iota((32, 128), 1) < 64
    for pair in range(slots // 2):
        left_z = z_scr[jnp.clip(src_s[0, 2 * pair], 0, SUB - 1)]
        right_z = pltpu.roll(z_scr[jnp.clip(src_s[0, 2 * pair + 1], 0, SUB - 1)], 64, 1)
        d, j = pair // (cap // 2), pair % (cap // 2)
        send[d, 32 * j:32 * j + 32, :] = jnp.where(low_half, left_z, right_z).astype(BF16)

    pl.semaphore_wait(barrier, n_span + n_freq - 2)
    moves = []
    for o in range(1, n_span):
        to = lax.rem(me_s + o, n_span)
        move = pltpu.make_async_remote_copy(
            src_ref=send.at[to], dst_ref=got.at[o - 1], send_sem=a_send.at[o - 1],
            recv_sem=a_recv.at[o - 1], device_id=(to, me_f), device_id_type=MESH,
        )
        move.start()
        moves.append(move)

    channels = CH_DEV * n_freq
    lane = iota((1, 128), 1)
    lane_a = lax.rem(lane, 32).astype(F32)
    cell_row = iota((TILE, 128), 0).astype(F32)
    cell_col = iota((32, 128), 1).astype(F32)

    def place(block):
        wide = jnp.dot(block[0:data_rows, :], repeat_ref[...], preferred_element_type=F32)
        info = block[data_rows:, :].astype(F32)
        rhs = []
        for i in range(cap):
            j, h = i // 2, i % 2
            off = cell_col - jnp.broadcast_to(info[i:i + 1, :], (32, 128))
            inside = (off >= 0.0) & (off < 32.0)
            part = wide[32 * j:32 * j + 32, 256 * h:256 * h + 256]
            rhs.append(
                jnp.concatenate(
                    [jnp.where(inside, part[:, :128], 0.0), jnp.where(inside, part[:, 128:], 0.0)],
                    1,
                )
            )
        rhs = jnp.concatenate(rhs, 0).astype(BF16)
        terms = [[], [], []]
        for j in range(lanes // 128):
            at = 8 + 4 * j
            hit = cell_row == info[at:at + 1, :] + lane_a
            valid = info[at + 1:at + 2, :]
            chan = info[at + 2:at + 3, :] + (me_f * CH_DEV).astype(F32)
            xval = valid * ((2.0 * chan + 1.0 - channels) / channels)
            high = xval.astype(BF16).astype(F32)
            for t, val in enumerate([valid, high, xval - high]):
                terms[t].append(jnp.where(hit, jnp.broadcast_to(val, (TILE, 128)), 0.0))
        used = terms[:2] if channels & (channels - 1) == 0 and channels <= 256 else terms
        lhs = jnp.concatenate([jnp.concatenate(t, 1) for t in used], 0).astype(BF16)
        res = jnp.dot(lhs, rhs, preferred_element_type=F32)
        if len(used) == 3:
            res = jnp.concatenate([res[:TILE], res[TILE:2 * TILE] + res[2 * TILE:]], 0)
        return res

    acc = place(send.at[me_s])
    for o in range(1, n_span):
        moves[o - 1].wait_recv()
        acc = acc + place(got.at[o - 1])

    if n_freq * rows_per > 4 * TILE:
        pad = n_freq * rows_per - 4 * TILE
        acc_scr[4 * TILE:, :] = jnp.zeros((pad, 128), F32)
        rs_send[4 * TILE:, :] = jnp.zeros((pad, 128), BF16)
    for t in range(NT):
        for c in range(2):
            part = acc[t * TILE:(t + 1) * TILE, c * 128:(c + 1) * 128]
            at = (2 * t + c) * TILE
            acc_scr[at:at + TILE, :] = part
            rs_send[at:at + TILE, :] = part.astype(BF16)

    sums = []
    for o in range(1, n_freq):
        to = lax.rem(me_f + o, n_freq)
        move = pltpu.make_async_remote_copy(
            src_ref=rs_send.at[pl.ds(pl.multiple_of(to * rows_per, rows_per), rows_per)],
            dst_ref=rs_got.at[o - 1], send_sem=r_send.at[o - 1], recv_sem=r_recv.at[o - 1],
            device_id=(me_s, to), device_id_type=MESH,
        )
        move.start()
        sums.append(move)
    own_rows = pl.ds(pl.multiple_of(me_f * rows_per, rows_per), rows_per)
    total = acc_scr[own_rows, :]
    for o in range(1, n_freq):
        sums[o - 1].wait_recv()
        total = total + rs_got[o - 1].astype(F32)
    scale = TILE / (32.0 * math.sqrt(n_freq * SUB))
    ag_send[...] = (total * scale).astype(BF16)
    gathers = []
    for o in range(1, n_freq):
        to = lax.rem(me_f + o, n_freq)
        move = pltpu.make_async_remote_copy(
            src_ref=ag_send, dst_ref=ag_got.at[o - 1], send_sem=g_send.at[o - 1],
            recv_sem=g_recv.at[o - 1], device_id=(me_s, to), device_id_type=MESH,
        )
        move.start()
        gathers.append(move)
    out_ref[own_rows, :] = ag_send[...].astype(F32)
    for o in range(1, n_freq):
        gathers[o - 1].wait_recv()
        frm = lax.rem(me_f - o + n_freq, n_freq)
        out_ref[pl.ds(pl.multiple_of(frm * rows_per, rows_per), rows_per), :] = ag_got[
            o - 1
        ].astype(F32)
    for move in moves + sums + gathers:
        move.wait_send()


def body(visibilities, coords, vis_counts, cover_tile, offsets, channel, taper):
    n_span = lax.axis_size("span")
    n_freq = lax.axis_size("freq")
    sub = visibilities.shape[1]
    kk = visibilities.shape[-1]
    cap = max(4, 2 * sub // n_span)
    slots = n_span * cap
    rows_per = -(-4 * TILE // n_freq // 16) * 16
    while rows_per * n_freq < 4 * TILE:
        rows_per += 16
    row, col, chan = offsets[:, :, 0], offsets[:, :, 1], channel
    one, tile = jnp.ones_like(chan), cover_tile[:, :, 0]
    none = jnp.zeros((7, sub), jnp.int32)
    meta = jnp.concatenate(
        [row, one, chan, tile, row, one, chan, col, vis_counts, none], axis=0
    )
    dma = pltpu.SemaphoreType.DMA
    block = cap * 16 + 16
    out = pl.pallas_call(
        functools.partial(kernel, n_span, n_freq, cap, rows_per),
        out_shape=jax.ShapeDtypeStruct((n_freq * rows_per, 128), F32),
        in_specs=[pl.BlockSpec(memory_space=pltpu.VMEM)] * 7,
        out_specs=pl.BlockSpec(memory_space=pltpu.VMEM),
        scratch_shapes=[
            pltpu.VMEM((12, sub, kk), F32),
            pltpu.VMEM((14, sub, kk), F32),
            pltpu.VMEM((sub * 64, 64), BF16),
            pltpu.VMEM((sub * 64, 128), BF16),
            pltpu.VMEM((sub, 32, 128), F32),
            pltpu.VMEM((8, 128), jnp.int32),
            pltpu.SMEM((8, 128), jnp.int32),
            pltpu.VMEM((n_span, block, 128), BF16),
            pltpu.VMEM((n_span - 1, block, 128), BF16),
            pltpu.VMEM((n_freq * rows_per, 128), F32),
            pltpu.VMEM((n_freq * rows_per, 128), BF16),
            pltpu.VMEM((n_freq - 1, rows_per, 128), BF16),
            pltpu.VMEM((rows_per, 128), BF16),
            pltpu.VMEM((n_freq - 1, rows_per, 128), BF16),
            dma(()),
            dma((n_span - 1,)), dma((n_span - 1,)),
            dma((n_freq - 1,)), dma((n_freq - 1,)),
            dma((n_freq - 1,)), dma((n_freq - 1,)),
        ],
        compiler_params=pltpu.CompilerParams(
            collective_id=0, has_side_effects=True, vmem_limit_bytes=32 * 1024 * 1024
        ),
    )(
        meta, coords.reshape(sub, 2 * kk), visibilities.reshape(sub, 2 * kk), taper,
        *[jnp.asarray(m) for m in dft_constants()],
    )
    return out[:4 * TILE].reshape(NT, 1, 2, TILE, TILE)


def solution(mesh):
    return jax.shard_map(
        body,
        mesh=mesh,
        in_specs=(
            P("freq", "span", None, None),
            P("freq", "span", None, None),
            P("freq", "span"),
            P("freq", "span", None),
            P("freq", "span", None),
            P("freq", "span"),
            P(),
        ),
        out_specs=P(None, "span", None, None, None),
        check_vma=False,
    )
```

profile of v0, /device:TPU:0, one launch (start us, length us, event | category | flops | bytes accessed | tf_op | source)
XLA Modules:
  0.0 27.9 jit_solution(9327125186071590581)
XLA Ops:
  0.0 0.0 copy-start.4
  0.0 0.8 %slice_bitcast_fusion = (s32[1,32]{1,0:T(1,128)S(1)}, s32[1,32]{1,0:T(1,128)S(1)}) fusion(s32[1,32,2]{1,2,0:T(2,128)} %param.14), kind=kLoop, calls=%fused_computation | loop fusion | bytes 512 | tf_op jit(solution)/shard_map/squeeze | solution.py:329
  0.8 1.4 %concatenate.3.meta_ref = s32[16,32]{1,0:T(8,128)S(1)} concatenate(s32[1,32]{1,0:T(1,128)S(1)} %get-tuple-element.6, s32[1,32]{1,0:T(1,128)S(1)} %broadcast_in_dim.6, s32[1,32]{1,0:T(1,128)} %param.15, s32[1,32]{1,0:T(1,128)} %bitcast.19, s32[1,32]{1,0:T(1,128)S(1)} %get-tuple-element.6, s32[1,32]{1,0:T(1,128)S(1)} %broadcast_in_dim.6, s32[1,32]{1,0:T(1,128)} %param.15, ...), dimensions={0} | concatenate | bytes 4096 | tf_op jit(solution)/shard_map/concatenate | solution.py:332
  2.2 0.8 %copy.13 = bf16[4,8,2,512]{3,1,2,0:T(8,128)(2,1)S(1)} copy(bf16[4,8,2,512]{3,2,1,0:T(2,128)(2,1)} %bitcast.18) | data formatting | bytes 131072
  3.0 0.0 copy-done.4
  3.0 0.0 copy-start
  3.1 0.0 copy-start.1
  3.1 0.0 copy-start.2
  3.1 0.0 copy-start.3
  3.1 0.8 %copy-done = bf16[128,512]{1,0:T(8,128)(2,1)S(1)} copy-done((bf16[128,512]{1,0:T(8,128)(2,1)S(1)}, bf16[128,512]{1,0:T(8,128)(2,1)}, u32[]{:S(2)}) %copy-start) | copy-done | bytes 131096
  4.0 0.0 copy-done.1
  4.0 0.0 copy-done.2
  4.0 0.0 copy-done.3
  4.0 23.2 %shard_map.100 = f32[512,128]{1,0:T(8,128)S(1)} custom-call(s32[16,32]{1,0:T(8,128)S(1)} %concatenate.3.meta_ref, f32[32,1024]{1,0:T(8,128)S(1)} %bitcast.15, bf16[32,1024]{1,0:T(8,128)(2,1)S(1)} %bitcast.16, f32[32,32]{1,0:T(8,128)S(1)} %copy-done.1, bf16[64,128]{1,0:T(8,128)(2,1)S(1)} %copy-done.3, bf16[64,64]{1,0:T(8,128)(2,1)S(1)} %copy-done.2, ...), custom_call_target="tpu_custom_call" | custom-call | tf_op jit(solution)/shard_map/pallas_call | solution.py:337
  27.2 0.7 %copy.15 = f32[2,1,2,128,128]{4,3,2,1,0:T(8,128)} copy(f32[2,1,2,128,128]{4,3,2,1,0:T(8,128)S(1)} %bitcast.14) | data formatting | bytes 524288
  (3 shorter events, 0.0 us)
Async XLA Ops:
  0.0 3.0 %copy-start.4 = (f32[1,32,2,512]{3,2,1,0:T(2,128)S(1)}, f32[1,32,2,512]{3,2,1,0:T(2,128)}, u32[]{:S(2)}) copy-start(f32[1,32,2,512]{3,2,1,0:T(2,128)} %param.11) | copy-start | bytes 393220
  3.0 0.9 %copy-start = (bf16[128,512]{1,0:T(8,128)(2,1)S(1)}, bf16[128,512]{1,0:T(8,128)(2,1)}, u32[]{:S(2)}) copy-start(bf16[128,512]{1,0:T(8,128)(2,1)} %constant.12.clone.repeat_ref) | copy-start | bytes 393220
  3.1 0.9 %copy-start.1 = (f32[32,32]{1,0:T(8,128)S(1)}, f32[32,32]{1,0:T(8,128)}, u32[]{:S(2)}) copy-start(f32[32,32]{1,0:T(8,128)} %taper_ref.1) | copy-start | bytes 12292
  3.1 0.9 %copy-start.2 = (bf16[64,64]{1,0:T(8,128)(2,1)S(1)}, bf16[64,64]{1,0:T(8,128)(2,1)}, u32[]{:S(2)}) copy-start(bf16[64,64]{1,0:T(8,128)(2,1)} %constant.11.clone.left_ref) | copy-start | bytes 24580
  3.1 0.9 %copy-start.3 = (bf16[64,128]{1,0:T(8,128)(2,1)S(1)}, bf16[64,128]{1,0:T(8,128)(2,1)}, u32[]{:S(2)}) copy-start(bf16[64,128]{1,0:T(8,128)(2,1)} %constant.10.clone.right_ref) | copy-start | bytes 49156
where the time goes:
time: 28.1 us; the launch traced here: 27.9 us
  Pallas kernels  23.2 us (83%)
  local copies, waits for them, and re-layouts  4.61 us (16%)
    pallas_call x1, Pallas kernels, body(): pl.pallas_call(functools.partial(kernel, n_span, n_freq, cap, rows_per),...  23.2 us
    unnamed x13, local copies, waits for them, and re-layouts  2.43 us
    concatenate x1, local copies, waits for them, and re-layouts, body(): jnp.concatenate([row, one, chan, tile, row, one, chan, col, vis_counts, n...  1.42 us
    squeeze x1, local copies, waits for them, and re-layouts, body(): row, col, chan = (offsets[:, :, 0], offsets[:, :, 1], channel)  0.76 us

commit v1 on v0

v1 whole, which is shorter than its diff:
```python
import functools
import math

import jax
import jax.numpy as jnp
from jax import lax
from jax.experimental import pallas as pl
from jax.experimental.pallas import tpu as pltpu
from jax.sharding import PartitionSpec as P

TILE = 128
NT = 2
CH_DEV = 16
SUB = 32
MESH = pl.DeviceIdType.MESH
F32 = jnp.float32
BF16 = jnp.bfloat16


def iota(shape, axis):
    return lax.broadcasted_iota(jnp.int32, shape, axis)


def unit_phase(turns):
    frac = turns - jnp.round(turns)
    half = frac * math.pi
    sq = half * half
    sin_h = sum_poly(sq, [(-1.0) ** n / math.factorial(2 * n + 1) for n in range(7)]) * half
    cos_h = sum_poly(sq, [(-1.0) ** n / math.factorial(2 * n) for n in range(8)])
    return 1.0 - 2.0 * sin_h * sin_h, 2.0 * sin_h * cos_h


def sum_poly(x, coefs):
    total = jnp.full_like(x, coefs[-1])
    for coef in coefs[-2::-1]:
        total = total * x + coef
    return total


def cmul(a, b):
    return a[0] * b[0] - a[1] * b[1], a[0] * b[1] + a[1] * b[0]


def kernel(
    n_span, n_freq, cap, rows_per, tile_ref, offs_ref, chan_ref, count_ref, coord_ref, vis_ref,
    taper_ref, out_ref, ea, eb, g_scr, y_scr, z_scr, rhs_scr, src_v, src_s, send, got, acc_scr,
    rs_send, rs_got, ag_send, ag_got, src_sem, a_send, a_recv, r_send, r_recv, g_send, g_recv,
):
    me_s, me_f = lax.axis_index("span"), lax.axis_index("freq")
    barrier = pltpu.get_barrier_semaphore()
    for o in range(1, n_span):
        pl.semaphore_signal(
            barrier, inc=1, device_id=(lax.rem(me_s + o, n_span), me_f), device_id_type=MESH
        )
    for o in range(1, n_freq):
        pl.semaphore_signal(
            barrier, inc=1, device_id=(me_s, lax.rem(me_f + o, n_freq)), device_id_type=MESH
        )

    kk = coord_ref.shape[2]
    lanes = cap * 32
    data_rows = cap * 16
    slots = n_span * cap

    tile_l, chan_l = tile_ref[...].astype(F32), chan_ref[...].astype(F32)
    row_l, col_l = offs_ref[0:1, :].astype(F32), offs_ref[1:2, :].astype(F32)
    count_l = count_ref[...].astype(F32)
    kind = lax.rem(iota((16, SUB), 0), 4)
    meta = jnp.where(
        kind == 0, jnp.broadcast_to(row_l, (16, SUB)),
        jnp.where(kind == 1, 1.0, jnp.broadcast_to(chan_l, (16, SUB))),
    )
    eye = iota((SUB, SUB), 0) == iota((SUB, SUB), 1)

    def to_rows(row):
        return jnp.sum(
            jnp.where(eye, jnp.broadcast_to(row, (SUB, SUB)), 0.0), axis=1, keepdims=True
        )

    dest_l = tile_l
    dest_s = to_rows(dest_l)
    same = jnp.broadcast_to(dest_l, (SUB, SUB)) == dest_s
    lower = iota((SUB, SUB), 1) < iota((SUB, SUB), 0)
    upper = iota((SUB, SUB), 0) < iota((SUB, SUB), 1)
    rank_s = jnp.sum(jnp.where(same & lower, 1.0, 0.0), axis=1, keepdims=True)
    rank_l = jnp.sum(jnp.where(same & upper, 1.0, 0.0), axis=0, keepdims=True)
    slot_s = (dest_s * cap + rank_s).astype(jnp.int32)
    slot_l = (dest_l * cap + rank_l).astype(jnp.int32)
    hot = jnp.broadcast_to(slot_s, (SUB, 128)) == iota((SUB, 128), 1)
    src = jnp.sum(jnp.where(hot, iota((SUB, 128), 0).astype(F32), 0.0), axis=0, keepdims=True)
    turn_s = to_rows(col_l)
    turn_s = turn_s - 32.0 * jnp.floor(turn_s * (1.0 / 32.0))
    turn = jnp.sum(
        jnp.where(iota((SUB, 128), 0) == iota((SUB, 128), 1), turn_s, 0.0), axis=0, keepdims=True
    )
    src_v[...] = jnp.where(
        iota((8, 128), 0) == 0, jnp.broadcast_to(src, (8, 128)), jnp.broadcast_to(turn, (8, 128))
    ).astype(jnp.int32)
    src_copy = pltpu.make_async_copy(src_v, src_s, src_sem)
    src_copy.start()
    col_s = to_rows(col_l)
    count_s = to_rows(count_l)
    hot_t = jnp.broadcast_to(slot_l, (slots, SUB)) == iota((slots, SUB), 0)
    col_splat = jnp.dot(
        jnp.where(hot_t, 1.0, 0.0).astype(BF16),
        jnp.broadcast_to(col_s, (SUB, 128)).astype(BF16),
        preferred_element_type=F32,
    )
    hot_x = jnp.broadcast_to(slot_s, (SUB, slots * 32)) == iota((SUB, slots * 32), 1) // 32
    spread_meta = jnp.dot(
        meta.astype(BF16), jnp.where(hot_x, 1.0, 0.0).astype(BF16), preferred_element_type=F32
    )
    eight = iota((8, 128), 0)
    for d in range(n_span):
        cols = col_splat[d * cap:(d + 1) * cap]
        if cap < 8:
            cols = jnp.concatenate([cols, jnp.zeros((8 - cap, 128), F32)], 0)
        info = spread_meta[0:8, d * lanes:d * lanes + 128]
        if lanes > 128:
            info = jnp.where(eight < 4, info, spread_meta[0:8, d * lanes + 128:d * lanes + 256])
        send[d, data_rows:, :] = jnp.concatenate([cols, info], 0).astype(BF16)

    def powers(turns):
        e1 = unit_phase(turns)
        e2 = cmul(e1, e1)
        e3 = cmul(e2, e1)
        e4 = cmul(e2, e2)
        e8 = cmul(e4, e4)
        e16 = cmul(e8, e8)
        return e1, e2, e3, e4, e8, e16

    def phases(i, carry):
        rows = pl.ds(pl.multiple_of(i * 8, 8), 8)
        for n, val in enumerate(powers(coord_ref[rows, 0, :] * (-1.0 / 32.0))):
            ea[2 * n, rows, :] = val[0]
            ea[2 * n + 1, rows, :] = val[1]
        return carry

    lax.fori_loop(0, SUB // 8, phases, 0)
    e1, e2, e3, e4, e8, e16 = powers(coord_ref[:, 1, :] * (-1.0 / 32.0))
    live = jnp.where(
        iota((SUB, kk), 1).astype(F32) < jnp.broadcast_to(count_s, (SUB, kk)),
        1.0 / math.sqrt(kk), 0.0,
    )
    vis = vis_ref[...].astype(F32)
    w0 = (vis[:, 0, :] * live, vis[:, 1, :] * live)
    for n, val in enumerate([w0, cmul(w0, e1), cmul(w0, e2), cmul(w0, e3), e4, e8, e16]):
        eb[2 * n] = val[0]
        eb[2 * n + 1] = val[1]

    sub8 = iota((8, kk), 0)
    bit0, bit1, bit2 = lax.rem(sub8, 2) == 1, lax.rem(sub8 // 2, 2) == 1, sub8 >= 4
    taper = taper_ref[...]
    taper = jnp.concatenate([taper, taper], 1)
    taper = jnp.concatenate([taper, taper], 0)
    taper = jnp.concatenate([taper, taper], 1)
    low_half64 = iota((64, 128), 1) < 64

    def expand(rows4, e4, e8, e16):
        low = [
            jnp.where(
                bit1, jnp.where(bit0, rows4[3][c], rows4[2][c]),
                jnp.where(bit0, rows4[1][c], rows4[0][c]),
            )
            for c in range(2)
        ]
        base = cmul(low, (jnp.where(bit2, e4[0], 1.0), jnp.where(bit2, e4[1], 0.0)))
        rr, ii = base[0] * e8[0], base[1] * e8[1]
        ri, ir = base[0] * e8[1], base[1] * e8[0]
        first = (base[0] * e16[0] + base[1] * e16[1], base[1] * e16[0] - base[0] * e16[1])
        blocks = [first, (rr + ii, ir - ri), base, (rr - ii, ri + ir)]
        return jnp.concatenate(
            [b[0] for b in blocks] + [b[1] for b in blocks], 0
        ).astype(BF16)

    def one_sub(s, carry):
        def row(ref, n):
            return tuple(
                jnp.broadcast_to(ref[2 * n + c, pl.ds(s, 1), :], (8, kk)) for c in range(2)
            )

        one = (jnp.ones((8, kk), F32), jnp.zeros((8, kk), F32))
        a_cat = expand([one] + [row(ea, n) for n in range(3)], *[row(ea, n) for n in range(3, 6)])
        b_cat = expand([row(eb, n) for n in range(4)], *[row(eb, n) for n in range(4, 7)])
        grid = lax.dot_general(
            a_cat, b_cat, (((1,), (1,)), ((), ())), preferred_element_type=F32
        )
        wide = jnp.concatenate([grid, grid], 1) * taper
        high = wide.astype(BF16)
        rest = (wide - high.astype(F32)).astype(BF16)
        rows = pl.ds(pl.multiple_of(s * 64, 64), 64)
        g_scr[rows, 0:128] = high
        g_scr[rows, 128:256] = rest
        return carry

    lax.fori_loop(0, SUB, one_sub, 0, unroll=4)

    def turns_of(rows, cols):
        prod = (lax.rem(rows, 32) - 16) * (lax.rem(cols, 32) - 16)
        return prod.astype(F32) * (-1.0 / 32.0)

    def quarter(n):
        return n.astype(F32) * 0.25

    rows, cols = iota((64, 128), 0), iota((64, 128), 1)
    right = unit_phase(
        turns_of(rows, cols) + quarter(cols // 64 + rows // 32 - lax.rem(cols // 32, 2))
    )[0]
    right_h = right.astype(BF16)
    right_l = (right - right_h.astype(F32)).astype(BF16)
    right = jnp.concatenate([right_h, right_l, right_h, jnp.zeros((64, 128), BF16)], 0)
    rows, cols = iota((64, 64), 0), iota((64, 64), 1)
    left = unit_phase(turns_of(rows, cols) + quarter(cols // 32 - rows // 32))[0]
    left = (left * (1.0 / 32.0)).astype(BF16)
    rows, cols = iota((128, 512), 0), iota((128, 512), 1)
    repeat = jnp.where(
        (rows // 32 == cols // 128) & (lax.rem(rows, 32) == lax.rem(cols, 32)), 1.0, 0.0
    ).astype(BF16)

    y_scr[...] = jnp.dot(g_scr[...], right, preferred_element_type=F32).astype(BF16)
    lane32 = lax.rem(iota((32, 128), 1), 32)
    src_copy.wait()

    def second(s, carry):
        part = jnp.dot(
            left, y_scr[pl.ds(pl.multiple_of(s * 64, 64), 64), :], preferred_element_type=F32
        )
        sub = part[:32] + pltpu.roll(part[32:], 64, 1)
        turn = jnp.clip(src_s[1, s], 0, 31)
        z_scr[s] = jnp.where(
            lane32 >= turn, pltpu.roll(sub, turn, 1), pltpu.roll(sub, turn + 96, 1)
        )
        return carry

    lax.fori_loop(0, SUB, second, 0, unroll=8)

    low_half = iota((32, 128), 1) < 64
    for pair in range(slots // 2):
        left_z = z_scr[jnp.clip(src_s[0, 2 * pair], 0, SUB - 1)]
        right_z = pltpu.roll(z_scr[jnp.clip(src_s[0, 2 * pair + 1], 0, SUB - 1)], 64, 1)
        d, j = pair // (cap // 2), pair % (cap // 2)
        send[d, 32 * j:32 * j + 32, :] = jnp.where(low_half, left_z, right_z).astype(BF16)

    pl.semaphore_wait(barrier, n_span + n_freq - 2)
    moves = []
    for o in range(1, n_span):
        to = lax.rem(me_s + o, n_span)
        move = pltpu.make_async_remote_copy(
            src_ref=send.at[to], dst_ref=got.at[o - 1], send_sem=a_send.at[o - 1],
            recv_sem=a_recv.at[o - 1], device_id=(to, me_f), device_id_type=MESH,
        )
        move.start()
        moves.append(move)

    channels = CH_DEV * n_freq
    lane = iota((1, 128), 1)
    lane_a = lax.rem(lane, 32).astype(F32)
    cell_row = iota((TILE, 128), 0).astype(F32)
    cell_col = iota((32, 128), 1).astype(F32)

    def widen(block, n):
        wide = jnp.dot(block[0:data_rows, :], repeat, preferred_element_type=F32)
        info = block[data_rows:, :].astype(F32)
        for i in range(cap):
            j, h = i // 2, i % 2
            off = cell_col - jnp.broadcast_to(info[i:i + 1, :], (32, 128))
            inside = (off >= 0.0) & (off < 32.0)
            part = wide[32 * j:32 * j + 32, 256 * h:256 * h + 256]
            rhs_scr[n, 32 * i:32 * i + 32, 0:128] = jnp.where(
                inside, part[:, :128], 0.0
            ).astype(BF16)
            rhs_scr[n, 32 * i:32 * i + 32, 128:256] = jnp.where(
                inside, part[:, 128:], 0.0
            ).astype(BF16)

    exact = channels & (channels - 1) == 0 and channels <= 256

    def weigh(block, n, term):
        info = block[data_rows:, :].astype(F32)
        high, low = [], []
        for j in range(lanes // 128):
            at = 8 + 4 * j
            hit = cell_row == info[at:at + 1, :] + lane_a
            val = info[at + 1:at + 2, :]
            if term == 1:
                chan = info[at + 2:at + 3, :] + (me_f * CH_DEV).astype(F32)
                val = val * ((2.0 * chan + 1.0 - channels) / channels)
            cut = val.astype(BF16).astype(F32)
            high.append(jnp.where(hit, jnp.broadcast_to(cut, (TILE, 128)), 0.0).astype(BF16))
            low.append(jnp.where(hit, jnp.broadcast_to(val - cut, (TILE, 128)), 0.0).astype(BF16))
        res = jnp.dot(jnp.concatenate(high, 1), rhs_scr[n], preferred_element_type=F32)
        if term == 1 and not exact:
            res = res + jnp.dot(jnp.concatenate(low, 1), rhs_scr[n], preferred_element_type=F32)
        return res

    blocks = [send.at[me_s]] + [got.at[o - 1] for o in range(1, n_span)]
    acc = None
    for n, block in enumerate(blocks):
        if n:
            moves[n - 1].wait_recv()
        widen(block, n)
        res = weigh(block, n, 0)
        acc = res if acc is None else acc + res

    def peer_rows(place):
        return pl.ds(pl.multiple_of(place * rows_per, rows_per), rows_per)

    half = 2 * TILE
    pad = n_freq * rows_per - half

    def scatter(acc, term):
        if pad:
            acc_scr[term, half:, :] = jnp.zeros((pad, 128), F32)
            rs_send[term, half:, :] = jnp.zeros((pad, 128), BF16)
        for c in range(2):
            part = acc[:, c * 128:(c + 1) * 128]
            acc_scr[term, c * TILE:(c + 1) * TILE, :] = part
            rs_send[term, c * TILE:(c + 1) * TILE, :] = part.astype(BF16)
        started = []
        for o in range(1, n_freq):
            to = lax.rem(me_f + o, n_freq)
            move = pltpu.make_async_remote_copy(
                src_ref=rs_send.at[term, peer_rows(to)], dst_ref=rs_got.at[term, o - 1],
                send_sem=r_send.at[term, o - 1], recv_sem=r_recv.at[term, o - 1],
                device_id=(me_s, to), device_id_type=MESH,
            )
            move.start()
            started.append(move)
        return started

    sums = [scatter(acc, 0)]
    acc = None
    for n, block in enumerate(blocks):
        res = weigh(block, n, 1)
        acc = res if acc is None else acc + res
    sums.append(scatter(acc, 1))

    scale = TILE / (32.0 * math.sqrt(n_freq * SUB))
    gathers = []
    for term in range(NT):
        total = acc_scr[term, peer_rows(me_f), :]
        for o in range(1, n_freq):
            sums[term][o - 1].wait_recv()
            total = total + rs_got[term, o - 1].astype(F32)
        ag_send[term] = (total * scale).astype(BF16)
        started = []
        for o in range(1, n_freq):
            to = lax.rem(me_f + o, n_freq)
            move = pltpu.make_async_remote_copy(
                src_ref=ag_send.at[term], dst_ref=ag_got.at[term, o - 1],
                send_sem=g_send.at[term, o - 1], recv_sem=g_recv.at[term, o - 1],
                device_id=(me_s, to), device_id_type=MESH,
            )
            move.start()
            started.append(move)
        gathers.append(started)
        out_ref[term, peer_rows(me_f), :] = ag_send[term].astype(F32)
    for term in range(NT):
        for o in range(1, n_freq):
            gathers[term][o - 1].wait_recv()
            frm = lax.rem(me_f - o + n_freq, n_freq)
            out_ref[term, peer_rows(frm), :] = ag_got[term, o - 1].astype(F32)
    for move in moves + sums[0] + sums[1] + gathers[0] + gathers[1]:
        move.wait_send()


def body(visibilities, coords, vis_counts, cover_tile, offsets, channel, taper):
    n_span = lax.axis_size("span")
    n_freq = lax.axis_size("freq")
    sub = visibilities.shape[1]
    kk = visibilities.shape[-1]
    cap = max(4, 2 * sub // n_span)
    rows_per = -(-2 * TILE // (16 * n_freq)) * 16
    dma = pltpu.SemaphoreType.DMA
    block = cap * 16 + 16
    out = pl.pallas_call(
        functools.partial(kernel, n_span, n_freq, cap, rows_per),
        out_shape=jax.ShapeDtypeStruct((NT, n_freq * rows_per, 128), F32),
        in_specs=[pl.BlockSpec(memory_space=pltpu.VMEM)] * 7,
        out_specs=pl.BlockSpec(memory_space=pltpu.VMEM),
        scratch_shapes=[
            pltpu.VMEM((12, sub, kk), F32),
            pltpu.VMEM((14, sub, kk), F32),
            pltpu.VMEM((sub * 64, 256), BF16),
            pltpu.VMEM((sub * 64, 128), BF16),
            pltpu.VMEM((sub, 32, 128), F32),
            pltpu.VMEM((n_span, cap * 32, 256), BF16),
            pltpu.VMEM((8, 128), jnp.int32),
            pltpu.SMEM((8, 128), jnp.int32),
            pltpu.VMEM((n_span, block, 128), BF16),
            pltpu.VMEM((n_span - 1, block, 128), BF16),
            pltpu.VMEM((NT, n_freq * rows_per, 128), F32),
            pltpu.VMEM((NT, n_freq * rows_per, 128), BF16),
            pltpu.VMEM((NT, n_freq - 1, rows_per, 128), BF16),
            pltpu.VMEM((NT, rows_per, 128), BF16),
            pltpu.VMEM((NT, n_freq - 1, rows_per, 128), BF16),
            dma(()),
            dma((n_span - 1,)), dma((n_span - 1,)),
            dma((NT, n_freq - 1)), dma((NT, n_freq - 1)),
            dma((NT, n_freq - 1)), dma((NT, n_freq - 1)),
        ],
        compiler_params=pltpu.CompilerParams(
            collective_id=0, has_side_effects=True, vmem_limit_bytes=32 * 1024 * 1024
        ),
    )(
        cover_tile[:, :, 0], offsets[0].T, channel, vis_counts, coords[0], visibilities[0], taper,
    )
    return out[:, :2 * TILE].reshape(NT, 1, 2, TILE, TILE)


def solution(mesh):
    return jax.shard_map(
        body,
        mesh=mesh,
        in_specs=(
            P("freq", "span", None, None),
            P("freq", "span", None, None),
            P("freq", "span"),
            P("freq", "span", None),
            P("freq", "span", None),
            P("freq", "span"),
            P(),
        ),
        out_specs=P(None, "span", None, None, None),
        check_vma=False,
    )
```

time: 28.1 us -> 28.4 us (1.011)
  Pallas kernels: 23.2 us -> 24.3 us
  local copies, waits for them, and re-layouts: 4.61 us -> 3.87 us
    unnamed x13 -> x15, local copies, waits for them, and re-layouts: 2.43 us -> 3.87 us
    concatenate x1 -> x0, local copies, waits for them, and re-layouts: 1.42 us -> none  [body(): jnp.concatenate([row, one, chan, tile, row, one, chan, col, vis_counts, n...]
    pallas_call x1, Pallas kernels: 23.2 us -> 24.3 us  [body(): pl.pallas_call(functools.partial(kernel, n_span, n_freq, cap, rows_per),...]
    squeeze x1 -> x0, local copies, waits for them, and re-layouts: 0.76 us -> none  [body(): row, col, chan = (offsets[:, :, 0], offsets[:, :, 1], channel)]
where the time goes in v1:
time: 28.4 us; the launch traced here: 28.2 us
  Pallas kernels  24.3 us (86%)
  local copies, waits for them, and re-layouts  3.87 us (14%)
    pallas_call x1, Pallas kernels, body(): pl.pallas_call(functools.partial(kernel, n_span, n_freq, cap, rows_per),...  24.3 us
    unnamed x15, local copies, waits for them, and re-layouts  3.87 us

profile of v1, /device:TPU:0, one launch (start us, length us, event | category | flops | bytes accessed | tf_op | source)
XLA Modules:
  0.0 28.2 jit_solution(1967338812924161890)
XLA Ops:
  0.0 0.0 copy-start.5
  0.0 0.0 copy-start.6
  0.0 0.0 copy-start.3
  0.0 0.0 copy-start.4
  0.0 0.6 %copy-done.5 = s32[1,32]{1,0:T(1,128)S(1)} copy-done((s32[1,32]{1,0:T(1,128)S(1)}, s32[1,32]{1,0:T(1,128)}, u32[]{:S(2)}) %copy-start.5) | copy-done | bytes 152
  0.7 0.0 copy-done.6
  0.7 0.0 copy-done.3
  0.7 0.0 copy-done.4
  0.7 0.0 copy-start
  0.7 0.9 %copy-done = f32[1,32,2,512]{3,2,1,0:T(2,128)S(1)} copy-done((f32[1,32,2,512]{3,2,1,0:T(2,128)S(1)}, f32[1,32,2,512]{3,2,1,0:T(2,128)}, u32[]{:S(2)}) %copy-start) | copy-done | bytes 131096
  1.6 0.0 copy-start.1
  1.6 0.8 %copy-done.1 = bf16[1,32,2,512]{3,2,1,0:T(2,128)(2,1)S(1)} copy-done((bf16[1,32,2,512]{3,2,1,0:T(2,128)(2,1)S(1)}, bf16[1,32,2,512]{3,2,1,0:T(2,128)(2,1)}, u32[]{:S(2)}) %copy-start.1) | copy-done | bytes 65560
  2.5 0.0 copy-start.2
  2.5 0.7 %copy-done.2 = f32[32,32]{1,0:T(8,128)S(1)} copy-done((f32[32,32]{1,0:T(8,128)S(1)}, f32[32,32]{1,0:T(8,128)}, u32[]{:S(2)}) %copy-start.2) | copy-done | bytes 4120
  3.2 24.3 %shard_map.73 = f32[2,256,128]{2,1,0:T(8,128)S(1)} custom-call(s32[1,32]{1,0:T(1,128)S(1)} %bitcast.13, s32[2,32]{1,0:T(2,128)S(1)} %bitcast.12, s32[1,32]{1,0:T(1,128)S(1)} %copy-done.5, s32[1,32]{1,0:T(1,128)S(1)} %copy-done.6, f32[32,2,512]{2,1,0:T(2,128)S(1)} %bitcast.10, bf16[32,2,512]{2,1,0:T(2,128)(2,1)S(1)} %bitcast.11, f32[32,32]{1,0:T(8,128)S(1)} %copy-done.2), custom_call_target="tpu_custom_call" | custom-call | tf_op jit(solution)/shard_map/pallas_call | solution.py:376
  27.5 0.7 %copy.10 = f32[2,1,2,128,128]{4,3,2,1,0:T(8,128)} copy(f32[2,1,2,128,128]{4,3,2,1,0:T(8,128)S(1)} %bitcast.9) | data formatting | bytes 524288
Async XLA Ops:
  0.0 0.7 %copy-start.5 = (s32[1,32]{1,0:T(1,128)S(1)}, s32[1,32]{1,0:T(1,128)}, u32[]{:S(2)}) copy-start(s32[1,32]{1,0:T(1,128)} %chan_ref.1) | copy-start | bytes 388
  0.0 0.7 %copy-start.6 = (s32[1,32]{1,0:T(1,128)S(1)}, s32[1,32]{1,0:T(1,128)}, u32[]{:S(2)}) copy-start(s32[1,32]{1,0:T(1,128)} %count_ref.1) | copy-start | bytes 388
  0.0 0.7 %copy-start.3 = (s32[1,32,2]{1,2,0:T(2,128)S(1)}, s32[1,32,2]{1,2,0:T(2,128)}, u32[]{:S(2)}) copy-start(s32[1,32,2]{1,2,0:T(2,128)} %param.11) | copy-start | bytes 772
  0.0 0.7 %copy-start.4 = (s32[1,32,1]{1,2,0:T(1,128)S(1)}, s32[1,32,1]{1,2,0:T(1,128)}, u32[]{:S(2)}) copy-start(s32[1,32,1]{1,2,0:T(1,128)} %param.10) | copy-start | bytes 388
  0.7 0.9 %copy-start = (f32[1,32,2,512]{3,2,1,0:T(2,128)S(1)}, f32[1,32,2,512]{3,2,1,0:T(2,128)}, u32[]{:S(2)}) copy-start(f32[1,32,2,512]{3,2,1,0:T(2,128)} %param.8) | copy-start | bytes 393220
  1.6 0.8 %copy-start.1 = (bf16[1,32,2,512]{3,2,1,0:T(2,128)(2,1)S(1)}, bf16[1,32,2,512]{3,2,1,0:T(2,128)(2,1)}, u32[]{:S(2)}) copy-start(bf16[1,32,2,512]{3,2,1,0:T(2,128)(2,1)} %param.7) | copy-start | bytes 196612
  2.5 0.7 %copy-start.2 = (f32[32,32]{1,0:T(8,128)S(1)}, f32[32,32]{1,0:T(8,128)}, u32[]{:S(2)}) copy-start(f32[32,32]{1,0:T(8,128)} %taper_ref.1) | copy-start | bytes 12292

commit v2 on v1

--- a/solution.py
+++ b/solution.py
@@ -43,8 +43,9 @@
 
 def kernel(
     n_span, n_freq, cap, rows_per, tile_ref, offs_ref, chan_ref, count_ref, coord_ref, vis_ref,
-    taper_ref, out_ref, ea, eb, g_scr, y_scr, z_scr, rhs_scr, src_v, src_s, send, got, acc_scr,
-    rs_send, rs_got, ag_send, ag_got, src_sem, a_send, a_recv, r_send, r_recv, g_send, g_recv,
+    taper_ref, out_ref, tile_v, offs_v, chan_v, count_v, coord_v, vis_v, taper_v, in_sem, ea, eb,
+    ab_scr, g_scr, y_scr, z_scr, rhs_scr, src_v, src_s, send, got, acc_scr,
+    rs_send, rs_got, src_sem, a_send, a_recv, r_send, r_recv, g_send, g_recv,
 ):
     me_s, me_f = lax.axis_index("span"), lax.axis_index("freq")
     barrier = pltpu.get_barrier_semaphore()
@@ -57,6 +58,16 @@
             barrier, inc=1, device_id=(me_s, lax.rem(me_f + o, n_freq)), device_id_type=MESH
         )
 
+    hbm = [tile_ref, offs_ref, chan_ref, count_ref, coord_ref, vis_ref, taper_ref]
+    vmem = [tile_v, offs_v, chan_v, count_v, coord_v, vis_v, taper_v]
+    fetch = [
+        pltpu.make_async_copy(a, b, in_sem.at[n]) for n, (a, b) in enumerate(zip(hbm, vmem))
+    ]
+    for copy in fetch:
+        copy.start()
+    for copy in fetch[:4]:
+        copy.wait()
+    tile_ref, offs_ref, chan_ref, count_ref, coord_ref, vis_ref, taper_ref = vmem
     kk = coord_ref.shape[2]
     lanes = cap * 32
     data_rows = cap * 16
@@ -129,26 +140,26 @@
         e16 = cmul(e8, e8)
         return e1, e2, e3, e4, e8, e16
 
-    def phases(i, carry):
-        rows = pl.ds(pl.multiple_of(i * 8, 8), 8)
-        for n, val in enumerate(powers(coord_ref[rows, 0, :] * (-1.0 / 32.0))):
-            ea[2 * n, rows, :] = val[0]
-            ea[2 * n + 1, rows, :] = val[1]
-        return carry
-
-    lax.fori_loop(0, SUB // 8, phases, 0)
-    e1, e2, e3, e4, e8, e16 = powers(coord_ref[:, 1, :] * (-1.0 / 32.0))
-    live = jnp.where(
-        iota((SUB, kk), 1).astype(F32) < jnp.broadcast_to(count_s, (SUB, kk)),
-        1.0 / math.sqrt(kk), 0.0,
-    )
-    vis = vis_ref[...].astype(F32)
-    w0 = (vis[:, 0, :] * live, vis[:, 1, :] * live)
-    for n, val in enumerate([w0, cmul(w0, e1), cmul(w0, e2), cmul(w0, e3), e4, e8, e16]):
-        eb[2 * n] = val[0]
-        eb[2 * n + 1] = val[1]
-
-    sub8 = iota((8, kk), 0)
+    for copy in fetch[4:]:
+        copy.wait()
+    piece_lane = iota((8, 128), 1).astype(F32)
+    for g in range(SUB // 8):
+        rows = slice(8 * g, 8 * g + 8)
+        left_over = jnp.broadcast_to(count_s[rows], (8, 128)) - piece_lane
+        for kt in range(kk // 128):
+            cols = slice(128 * kt, 128 * kt + 128)
+            for n, val in enumerate(powers(coord_ref[rows, 0, cols] * (-1.0 / 32.0))):
+                ea[rows, 8 * n + kt, :] = val[0]
+                ea[rows, 8 * n + 4 + kt, :] = val[1]
+            e1, e2, e3, e4, e8, e16 = powers(coord_ref[rows, 1, cols] * (-1.0 / 32.0))
+            live = jnp.where(left_over > 128.0 * kt, 1.0 / math.sqrt(kk), 0.0)
+            vis = vis_ref[rows, :, cols].astype(F32)
+            w0 = (vis[:, 0, :] * live, vis[:, 1, :] * live)
+            for n, val in enumerate([w0, cmul(w0, e1), cmul(w0, e2), cmul(w0, e3), e4, e8, e16]):
+                eb[rows, 8 * n + kt, :] = val[0]
+                eb[rows, 8 * n + 4 + kt, :] = val[1]
+
+    sub8 = iota((8, 128), 0)
     bit0, bit1, bit2 = lax.rem(sub8, 2) == 1, lax.rem(sub8 // 2, 2) == 1, sub8 >= 4
     taper = taper_ref[...]
     taper = jnp.concatenate([taper, taper], 1)
@@ -169,31 +180,47 @@
         ri, ir = base[0] * e8[1], base[1] * e8[0]
         first = (base[0] * e16[0] + base[1] * e16[1], base[1] * e16[0] - base[0] * e16[1])
         blocks = [first, (rr + ii, ir - ri), base, (rr - ii, ri + ir)]
-        return jnp.concatenate(
-            [b[0] for b in blocks] + [b[1] for b in blocks], 0
-        ).astype(BF16)
-
-    def one_sub(s, carry):
-        def row(ref, n):
-            return tuple(
-                jnp.broadcast_to(ref[2 * n + c, pl.ds(s, 1), :], (8, kk)) for c in range(2)
+        return [
+            jnp.concatenate([blocks[2 * half][c], blocks[2 * half + 1][c]], 0).astype(BF16)
+            for c in range(2) for half in range(2)
+        ]
+
+    group = 8
+
+    def sub_group(i, carry):
+        for u in range(group):
+            s = i * group + u
+            for kt in range(kk // 128):
+                cols = slice(128 * kt, 128 * kt + 128)
+
+                def row(ref, n):
+                    return tuple(
+                        jnp.broadcast_to(ref[s, at:at + 1, :], (8, 128))
+                        for at in (8 * n + kt, 8 * n + 4 + kt)
+                    )
+
+                one = (jnp.ones((8, 128), F32), jnp.zeros((8, 128), F32))
+                a_rows = expand(
+                    [one] + [row(ea, n) for n in range(3)], *[row(ea, n) for n in range(3, 6)]
+                )
+                b_rows = expand(
+                    [row(eb, n) for n in range(4)], *[row(eb, n) for n in range(4, 7)]
+                )
+                for n in range(4):
+                    ab_scr[u, 0, 16 * n:16 * n + 16, cols] = a_rows[n]
+                    ab_scr[u, 1, 16 * n:16 * n + 16, cols] = b_rows[n]
+            grid = lax.dot_general(
+                ab_scr[u, 0], ab_scr[u, 1], (((1,), (1,)), ((), ())), preferred_element_type=F32
             )
-
-        one = (jnp.ones((8, kk), F32), jnp.zeros((8, kk), F32))
-        a_cat = expand([one] + [row(ea, n) for n in range(3)], *[row(ea, n) for n in range(3, 6)])
-        b_cat = expand([row(eb, n) for n in range(4)], *[row(eb, n) for n in range(4, 7)])
-        grid = lax.dot_general(
-            a_cat, b_cat, (((1,), (1,)), ((), ())), preferred_element_type=F32
-        )
-        wide = jnp.concatenate([grid, grid], 1) * taper
-        high = wide.astype(BF16)
-        rest = (wide - high.astype(F32)).astype(BF16)
-        rows = pl.ds(pl.multiple_of(s * 64, 64), 64)
-        g_scr[rows, 0:128] = high
-        g_scr[rows, 128:256] = rest
+            wide = jnp.concatenate([grid, grid], 1) * taper
+            high = wide.astype(BF16)
+            rest = (wide - high.astype(F32)).astype(BF16)
+            rows = pl.ds(pl.multiple_of(s * 64, 64), 64)
+            g_scr[rows, 0:128] = high
+            g_scr[rows, 128:256] = rest
         return carry
 
-    lax.fori_loop(0, SUB, one_sub, 0, unroll=4)
+    lax.fori_loop(0, SUB // group, sub_group, 0)
 
     def turns_of(rows, cols):
         prod = (lax.rem(rows, 32) - 16) * (lax.rem(cols, 32) - 16)
@@ -232,7 +259,7 @@
         )
         return carry
 
-    lax.fori_loop(0, SUB, second, 0, unroll=8)
+    lax.fori_loop(0, SUB, second, 0, unroll=16)
 
     low_half = iota((32, 128), 1) < 64
     for pair in range(slots // 2):
@@ -256,15 +283,15 @@
     lane = iota((1, 128), 1)
     lane_a = lax.rem(lane, 32).astype(F32)
     cell_row = iota((TILE, 128), 0).astype(F32)
-    cell_col = iota((32, 128), 1).astype(F32)
 
     def widen(block, n):
         wide = jnp.dot(block[0:data_rows, :], repeat, preferred_element_type=F32)
         info = block[data_rows:, :].astype(F32)
         for i in range(cap):
             j, h = i // 2, i % 2
-            off = cell_col - jnp.broadcast_to(info[i:i + 1, :], (32, 128))
-            inside = (off >= 0.0) & (off < 32.0)
+            off = piece_lane - jnp.broadcast_to(info[i:i + 1, :], (8, 128))
+            inside = jnp.where((off >= 0.0) & (off < 32.0), 1.0, 0.0)
+            inside = jnp.concatenate([inside] * 4, 0) > 0.5
             part = wide[32 * j:32 * j + 32, 256 * h:256 * h + 256]
             rhs_scr[n, 32 * i:32 * i + 32, 0:128] = jnp.where(
                 inside, part[:, :128], 0.0
@@ -295,12 +322,16 @@
 
     blocks = [send.at[me_s]] + [got.at[o - 1] for o in range(1, n_span)]
     acc = None
-    for n, block in enumerate(blocks):
-        if n:
-            moves[n - 1].wait_recv()
-        widen(block, n)
-        res = weigh(block, n, 0)
-        acc = res if acc is None else acc + res
+    starts = [0, 1, n_span // 2, n_span]
+    for first, last in zip(starts[:-1], starts[1:]):
+        for n in range(first, last):
+            if n:
+                moves[n - 1].wait_recv()
+        for n in range(first, last):
+            widen(blocks[n], n)
+        for n in range(first, last):
+            res = weigh(blocks[n], n, 0)
+            acc = res if acc is None else acc + res
 
     def peer_rows(place):
         return pl.ds(pl.multiple_of(place * rows_per, rows_per), rows_per)
@@ -342,24 +373,22 @@
         for o in range(1, n_freq):
             sums[term][o - 1].wait_recv()
             total = total + rs_got[term, o - 1].astype(F32)
-        ag_send[term] = (total * scale).astype(BF16)
+        mine = out_ref.at[term, peer_rows(me_f)]
+        mine[...] = (total * scale).astype(BF16)
         started = []
         for o in range(1, n_freq):
             to = lax.rem(me_f + o, n_freq)
             move = pltpu.make_async_remote_copy(
-                src_ref=ag_send.at[term], dst_ref=ag_got.at[term, o - 1],
+                src_ref=mine, dst_ref=mine,
                 send_sem=g_send.at[term, o - 1], recv_sem=g_recv.at[term, o - 1],
                 device_id=(me_s, to), device_id_type=MESH,
             )
             move.start()
             started.append(move)
         gathers.append(started)
-        out_ref[term, peer_rows(me_f), :] = ag_send[term].astype(F32)
     for term in range(NT):
         for o in range(1, n_freq):
             gathers[term][o - 1].wait_recv()
-            frm = lax.rem(me_f - o + n_freq, n_freq)
-            out_ref[term, peer_rows(frm), :] = ag_got[term, o - 1].astype(F32)
     for move in moves + sums[0] + sums[1] + gathers[0] + gathers[1]:
         move.wait_send()
 
@@ -375,12 +404,21 @@
     block = cap * 16 + 16
     out = pl.pallas_call(
         functools.partial(kernel, n_span, n_freq, cap, rows_per),
-        out_shape=jax.ShapeDtypeStruct((NT, n_freq * rows_per, 128), F32),
-        in_specs=[pl.BlockSpec(memory_space=pltpu.VMEM)] * 7,
+        out_shape=jax.ShapeDtypeStruct((NT, n_freq * rows_per, 128), BF16),
+        in_specs=[pl.BlockSpec(memory_space=pltpu.HBM)] * 7,
         out_specs=pl.BlockSpec(memory_space=pltpu.VMEM),
         scratch_shapes=[
-            pltpu.VMEM((12, sub, kk), F32),
-            pltpu.VMEM((14, sub, kk), F32),
+            pltpu.VMEM((1, sub), jnp.int32),
+            pltpu.VMEM((2, sub), jnp.int32),
+            pltpu.VMEM((1, sub), jnp.int32),
+            pltpu.VMEM((1, sub), jnp.int32),
+            pltpu.VMEM((sub, 2, kk), F32),
+            pltpu.VMEM((sub, 2, kk), BF16),
+            pltpu.VMEM((32, 32), F32),
+            dma((7,)),
+            pltpu.VMEM((sub, 48, 128), F32),
+            pltpu.VMEM((sub, 56, 128), F32),
+            pltpu.VMEM((8, 2, 64, kk), BF16),
             pltpu.VMEM((sub * 64, 256), BF16),
             pltpu.VMEM((sub * 64, 128), BF16),
             pltpu.VMEM((sub, 32, 128), F32),
@@ -392,20 +430,18 @@
             pltpu.VMEM((NT, n_freq * rows_per, 128), F32),
             pltpu.VMEM((NT, n_freq * rows_per, 128), BF16),
             pltpu.VMEM((NT, n_freq - 1, rows_per, 128), BF16),
-            pltpu.VMEM((NT, rows_per, 128), BF16),
-            pltpu.VMEM((NT, n_freq - 1, rows_per, 128), BF16),
             dma(()),
             dma((n_span - 1,)), dma((n_span - 1,)),
             dma((NT, n_freq - 1)), dma((NT, n_freq - 1)),
             dma((NT, n_freq - 1)), dma((NT, n_freq - 1)),
         ],
         compiler_params=pltpu.CompilerParams(
-            collective_id=0, has_side_effects=True, vmem_limit_bytes=32 * 1024 * 1024
+            collective_id=0, has_side_effects=True, vmem_limit_bytes=60 * 1024 * 1024
         ),
     )(
         cover_tile[:, :, 0], offsets[0].T, channel, vis_counts, coords[0], visibilities[0], taper,
     )
-    return out[:, :2 * TILE].reshape(NT, 1, 2, TILE, TILE)
+    return out[:, :2 * TILE].astype(F32).reshape(NT, 1, 2, TILE, TILE)
 
 
 def solution(mesh):

time: 28.4 us -> 28.6 us (level)
  local copies, waits for them, and re-layouts: 3.87 us -> 0 us
  Pallas kernels: 24.3 us -> 26.8 us
  other arithmetic: 0 us -> 1.63 us
    unnamed x15 -> x0, local copies, waits for them, and re-layouts: 3.87 us -> none
    pallas_call x1, Pallas kernels: 24.3 us -> 26.8 us  [body(): pl.pallas_call(functools.partial(kernel, n_span, n_freq, cap, rows_per),...]
    reshape x0 -> x1, other arithmetic: none -> 1.63 us  [body(): return out[:, :2 * TILE].astype(F32).reshape(NT, 1, 2, TILE, TILE)]
where the time goes in v2:
time: 28.6 us; the launch traced here: 28.5 us
  Pallas kernels  26.8 us (94%)
  other arithmetic  1.63 us (6%)
    pallas_call x1, Pallas kernels, body(): pl.pallas_call(functools.partial(kernel, n_span, n_freq, cap, rows_per),...  26.8 us
    reshape x1, other arithmetic, body(): return out[:, :2 * TILE].astype(F32).reshape(NT, 1, 2, TILE, TILE)  1.63 us

profile of v2, /device:TPU:0, one launch (start us, length us, event | category | flops | bytes accessed | tf_op | source)
XLA Modules:
  0.0 28.5 jit_solution(16570401265661745266)
XLA Ops:
  0.0 26.8 %shard_map.73 = bf16[2,256,128]{2,1,0:T(8,128)(2,1)} custom-call(s32[1,32]{1,0:T(1,128)} %bitcast.15, s32[2,32]{1,0:T(2,128)} %bitcast.14, s32[1,32]{1,0:T(1,128)} %chan_ref.1, s32[1,32]{1,0:T(1,128)} %count_ref.1, f32[32,2,512]{2,1,0:T(2,128)} %bitcast.12, bf16[32,2,512]{2,1,0:T(2,128)(2,1)} %bitcast.13, f32[32,32]{1,0:T(8,128)} %taper_ref.1), custom_call_target="tpu_custom_call" | custom-call | tf_op jit(solution)/shard_map/pallas_call | solution.py:405
  26.8 1.6 %convert.2 = f32[2,1,2,128,128]{4,3,2,1,0:T(8,128)} convert(bf16[2,1,2,128,128]{4,3,2,1,0:T(8,128)(2,1)} %bitcast.11) | non-fusion elementwise | flops 65536 | bytes 393216 | tf_op jit(solution)/shard_map/reshape | solution.py:444

commit v3 on v2

--- a/solution.py
+++ b/solution.py
@@ -44,7 +44,7 @@
 def kernel(
     n_span, n_freq, cap, rows_per, tile_ref, offs_ref, chan_ref, count_ref, coord_ref, vis_ref,
     taper_ref, out_ref, tile_v, offs_v, chan_v, count_v, coord_v, vis_v, taper_v, in_sem, ea, eb,
-    ab_scr, g_scr, y_scr, z_scr, rhs_scr, src_v, src_s, send, got, acc_scr,
+    ab_scr, g_scr, y_scr, z_scr, rhs_scr, src_v, src_s, send, got, tile_scr, count_scr, acc_scr,
     rs_send, rs_got, src_sem, a_send, a_recv, r_send, r_recv, g_send, g_recv,
 ):
     me_s, me_f = lax.axis_index("span"), lax.axis_index("freq")
@@ -76,7 +76,7 @@
     tile_l, chan_l = tile_ref[...].astype(F32), chan_ref[...].astype(F32)
     row_l, col_l = offs_ref[0:1, :].astype(F32), offs_ref[1:2, :].astype(F32)
     count_l = count_ref[...].astype(F32)
-    kind = lax.rem(iota((16, SUB), 0), 4)
+    kind = iota((16, SUB), 0) & 3
     meta = jnp.where(
         kind == 0, jnp.broadcast_to(row_l, (16, SUB)),
         jnp.where(kind == 1, 1.0, jnp.broadcast_to(chan_l, (16, SUB))),
@@ -117,7 +117,7 @@
         jnp.broadcast_to(col_s, (SUB, 128)).astype(BF16),
         preferred_element_type=F32,
     )
-    hot_x = jnp.broadcast_to(slot_s, (SUB, slots * 32)) == iota((SUB, slots * 32), 1) // 32
+    hot_x = jnp.broadcast_to(slot_s, (SUB, slots * 32)) == iota((SUB, slots * 32), 1) >> 5
     spread_meta = jnp.dot(
         meta.astype(BF16), jnp.where(hot_x, 1.0, 0.0).astype(BF16), preferred_element_type=F32
     )
@@ -143,9 +143,11 @@
     for copy in fetch[4:]:
         copy.wait()
     piece_lane = iota((8, 128), 1).astype(F32)
-    for g in range(SUB // 8):
-        rows = slice(8 * g, 8 * g + 8)
-        left_over = jnp.broadcast_to(count_s[rows], (8, 128)) - piece_lane
+    count_scr[...] = jnp.broadcast_to(count_s, (SUB, 128))
+
+    def phases(g, carry):
+        rows = pl.ds(pl.multiple_of(g * 8, 8), 8)
+        left_over = count_scr[rows, :] - piece_lane
         for kt in range(kk // 128):
             cols = slice(128 * kt, 128 * kt + 128)
             for n, val in enumerate(powers(coord_ref[rows, 0, cols] * (-1.0 / 32.0))):
@@ -158,9 +160,12 @@
             for n, val in enumerate([w0, cmul(w0, e1), cmul(w0, e2), cmul(w0, e3), e4, e8, e16]):
                 eb[rows, 8 * n + kt, :] = val[0]
                 eb[rows, 8 * n + 4 + kt, :] = val[1]
+        return carry
+
+    lax.fori_loop(0, SUB // 8, phases, 0)
 
     sub8 = iota((8, 128), 0)
-    bit0, bit1, bit2 = lax.rem(sub8, 2) == 1, lax.rem(sub8 // 2, 2) == 1, sub8 >= 4
+    bit0, bit1, bit2 = (sub8 & 1) == 1, (sub8 & 2) == 2, sub8 >= 4
     taper = taper_ref[...]
     taper = jnp.concatenate([taper, taper], 1)
     taper = jnp.concatenate([taper, taper], 0)
@@ -185,7 +190,7 @@
             for c in range(2) for half in range(2)
         ]
 
-    group = 8
+    group = 4
 
     def sub_group(i, carry):
         for u in range(group):
@@ -223,7 +228,7 @@
     lax.fori_loop(0, SUB // group, sub_group, 0)
 
     def turns_of(rows, cols):
-        prod = (lax.rem(rows, 32) - 16) * (lax.rem(cols, 32) - 16)
+        prod = ((rows & 31) - 16) * ((cols & 31) - 16)
         return prod.astype(F32) * (-1.0 / 32.0)
 
     def quarter(n):
@@ -231,21 +236,21 @@
 
     rows, cols = iota((64, 128), 0), iota((64, 128), 1)
     right = unit_phase(
-        turns_of(rows, cols) + quarter(cols // 64 + rows // 32 - lax.rem(cols // 32, 2))
+        turns_of(rows, cols) + quarter((cols >> 6) + (rows >> 5) - ((cols >> 5) & 1))
     )[0]
     right_h = right.astype(BF16)
     right_l = (right - right_h.astype(F32)).astype(BF16)
     right = jnp.concatenate([right_h, right_l, right_h, jnp.zeros((64, 128), BF16)], 0)
     rows, cols = iota((64, 64), 0), iota((64, 64), 1)
-    left = unit_phase(turns_of(rows, cols) + quarter(cols // 32 - rows // 32))[0]
+    left = unit_phase(turns_of(rows, cols) + quarter((cols >> 5) - (rows >> 5)))[0]
     left = (left * (1.0 / 32.0)).astype(BF16)
     rows, cols = iota((128, 512), 0), iota((128, 512), 1)
     repeat = jnp.where(
-        (rows // 32 == cols // 128) & (lax.rem(rows, 32) == lax.rem(cols, 32)), 1.0, 0.0
+        ((rows >> 5) == (cols >> 7)) & ((rows & 31) == (cols & 31)), 1.0, 0.0
     ).astype(BF16)
 
     y_scr[...] = jnp.dot(g_scr[...], right, preferred_element_type=F32).astype(BF16)
-    lane32 = lax.rem(iota((32, 128), 1), 32)
+    lane32 = iota((32, 128), 1) & 31
     src_copy.wait()
 
     def second(s, carry):
@@ -259,51 +264,52 @@
         )
         return carry
 
-    lax.fori_loop(0, SUB, second, 0, unroll=16)
+    lax.fori_loop(0, SUB, second, 0, unroll=8)
 
     low_half = iota((32, 128), 1) < 64
-    for pair in range(slots // 2):
-        left_z = z_scr[jnp.clip(src_s[0, 2 * pair], 0, SUB - 1)]
-        right_z = pltpu.roll(z_scr[jnp.clip(src_s[0, 2 * pair + 1], 0, SUB - 1)], 64, 1)
-        d, j = pair // (cap // 2), pair % (cap // 2)
-        send[d, 32 * j:32 * j + 32, :] = jnp.where(low_half, left_z, right_z).astype(BF16)
+
+    def fill(d, carry):
+        for j in range(cap // 2):
+            pair = d * (cap // 2) + j
+            left_z = z_scr[jnp.clip(src_s[0, 2 * pair], 0, SUB - 1)]
+            right_z = pltpu.roll(z_scr[jnp.clip(src_s[0, 2 * pair + 1], 0, SUB - 1)], 64, 1)
+            send[d, 32 * j:32 * j + 32, :] = jnp.where(low_half, left_z, right_z).astype(BF16)
+        return carry
+
+    lax.fori_loop(0, n_span, fill, 0)
 
     pl.semaphore_wait(barrier, n_span + n_freq - 2)
     moves = []
     for o in range(1, n_span):
         to = lax.rem(me_s + o, n_span)
         move = pltpu.make_async_remote_copy(
-            src_ref=send.at[to], dst_ref=got.at[o - 1], send_sem=a_send.at[o - 1],
-            recv_sem=a_recv.at[o - 1], device_id=(to, me_f), device_id_type=MESH,
+            src_ref=send.at[to], dst_ref=got.at[o], send_sem=a_send.at[o],
+            recv_sem=a_recv.at[o], device_id=(to, me_f), device_id_type=MESH,
         )
         move.start()
         moves.append(move)
 
     channels = CH_DEV * n_freq
     lane = iota((1, 128), 1)
-    lane_a = lax.rem(lane, 32).astype(F32)
+    lane_a = (lane & 31).astype(F32)
     cell_row = iota((TILE, 128), 0).astype(F32)
 
-    def widen(block, n):
-        wide = jnp.dot(block[0:data_rows, :], repeat, preferred_element_type=F32)
-        info = block[data_rows:, :].astype(F32)
+    def widen(n):
+        wide = jnp.dot(got[n, 0:data_rows, :], repeat, preferred_element_type=F32)
+        info = got[n, data_rows:, :].astype(F32)
         for i in range(cap):
             j, h = i // 2, i % 2
             off = piece_lane - jnp.broadcast_to(info[i:i + 1, :], (8, 128))
             inside = jnp.where((off >= 0.0) & (off < 32.0), 1.0, 0.0)
-            inside = jnp.concatenate([inside] * 4, 0) > 0.5
+            inside = jnp.concatenate([inside] * 4, 0)
             part = wide[32 * j:32 * j + 32, 256 * h:256 * h + 256]
-            rhs_scr[n, 32 * i:32 * i + 32, 0:128] = jnp.where(
-                inside, part[:, :128], 0.0
-            ).astype(BF16)
-            rhs_scr[n, 32 * i:32 * i + 32, 128:256] = jnp.where(
-                inside, part[:, 128:], 0.0
-            ).astype(BF16)
+            rhs_scr[n, 32 * i:32 * i + 32, 0:128] = (part[:, :128] * inside).astype(BF16)
+            rhs_scr[n, 32 * i:32 * i + 32, 128:256] = (part[:, 128:] * inside).astype(BF16)
 
     exact = channels & (channels - 1) == 0 and channels <= 256
 
-    def weigh(block, n, term):
-        info = block[data_rows:, :].astype(F32)
+    def weigh(n, term):
+        info = got[n, data_rows:, :].astype(F32)
         high, low = [], []
         for j in range(lanes // 128):
             at = 8 + 4 * j
@@ -320,18 +326,20 @@
             res = res + jnp.dot(jnp.concatenate(low, 1), rhs_scr[n], preferred_element_type=F32)
         return res
 
-    blocks = [send.at[me_s]] + [got.at[o - 1] for o in range(1, n_span)]
-    acc = None
-    starts = [0, 1, n_span // 2, n_span]
-    for first, last in zip(starts[:-1], starts[1:]):
-        for n in range(first, last):
-            if n:
-                moves[n - 1].wait_recv()
-        for n in range(first, last):
-            widen(blocks[n], n)
-        for n in range(first, last):
-            res = weigh(blocks[n], n, 0)
-            acc = res if acc is None else acc + res
+    got[0] = send[me_s]
+    widen(0)
+    tile_scr[...] = weigh(0, 0)
+
+    def receive(o, carry):
+        pltpu.make_async_remote_copy(
+            src_ref=send.at[0], dst_ref=got.at[o], send_sem=a_send.at[o], recv_sem=a_recv.at[o],
+            device_id=(lax.rem(me_s + 1, n_span), me_f), device_id_type=MESH,
+        ).wait_recv()
+        widen(o)
+        tile_scr[...] += weigh(o, 0)
+        return carry
+
+    lax.fori_loop(1, n_span, receive, 0)
 
     def peer_rows(place):
         return pl.ds(pl.multiple_of(place * rows_per, rows_per), rows_per)
@@ -339,7 +347,8 @@
     half = 2 * TILE
     pad = n_freq * rows_per - half
 
-    def scatter(acc, term):
+    def scatter(term):
+        acc = tile_scr[...]
         if pad:
             acc_scr[term, half:, :] = jnp.zeros((pad, 128), F32)
             rs_send[term, half:, :] = jnp.zeros((pad, 128), BF16)
@@ -359,12 +368,15 @@
             started.append(move)
         return started
 
-    sums = [scatter(acc, 0)]
-    acc = None
-    for n, block in enumerate(blocks):
-        res = weigh(block, n, 1)
-        acc = res if acc is None else acc + res
-    sums.append(scatter(acc, 1))
+    sums = [scatter(0)]
+    tile_scr[...] = weigh(0, 1)
+
+    def second_term(o, carry):
+        tile_scr[...] += weigh(o, 1)
+        return carry
+
+    lax.fori_loop(1, n_span, second_term, 0)
+    sums.append(scatter(1))
 
     scale = TILE / (32.0 * math.sqrt(n_freq * SUB))
     gathers = []
@@ -418,7 +430,7 @@
             dma((7,)),
             pltpu.VMEM((sub, 48, 128), F32),
             pltpu.VMEM((sub, 56, 128), F32),
-            pltpu.VMEM((8, 2, 64, kk), BF16),
+            pltpu.VMEM((4, 2, 64, kk), BF16),
             pltpu.VMEM((sub * 64, 256), BF16),
             pltpu.VMEM((sub * 64, 128), BF16),
             pltpu.VMEM((sub, 32, 128), F32),
@@ -426,12 +438,14 @@
             pltpu.VMEM((8, 128), jnp.int32),
             pltpu.SMEM((8, 128), jnp.int32),
             pltpu.VMEM((n_span, block, 128), BF16),
-            pltpu.VMEM((n_span - 1, block, 128), BF16),
+            pltpu.VMEM((n_span, block, 128), BF16),
+            pltpu.VMEM((TILE, 256), F32),
+            pltpu.VMEM((sub, 128), F32),
             pltpu.VMEM((NT, n_freq * rows_per, 128), F32),
             pltpu.VMEM((NT, n_freq * rows_per, 128), BF16),
             pltpu.VMEM((NT, n_freq - 1, rows_per, 128), BF16),
             dma(()),
-            dma((n_span - 1,)), dma((n_span - 1,)),
+            dma((n_span,)), dma((n_span,)),
             dma((NT, n_freq - 1)), dma((NT, n_freq - 1)),
             dma((NT, n_freq - 1)), dma((NT, n_freq - 1)),
         ],

time: 28.6 us -> 31.2 us (1.091)
  Pallas kernels: 26.8 us -> 29.4 us
    pallas_call x1, Pallas kernels: 26.8 us -> 29.4 us  [body(): pl.pallas_call(functools.partial(kernel, n_span, n_freq, cap, rows_per),...]
where the time goes in v3:
time: 31.2 us; the launch traced here: 31.1 us
  Pallas kernels  29.4 us (94%)
  other arithmetic  1.63 us (5%)
    pallas_call x1, Pallas kernels, body(): pl.pallas_call(functools.partial(kernel, n_span, n_freq, cap, rows_per),...  29.4 us
    reshape x1, other arithmetic, body(): return out[:, :2 * TILE].astype(F32).reshape(NT, 1, 2, TILE, TILE)  1.63 us

profile of v3, /device:TPU:0, one launch (start us, length us, event | category | flops | bytes accessed | tf_op | source)
XLA Modules:
  0.0 31.1 jit_solution(13878893158282975128)
XLA Ops:
  0.0 29.4 %shard_map.73 = bf16[2,256,128]{2,1,0:T(8,128)(2,1)} custom-call(s32[1,32]{1,0:T(1,128)} %bitcast.15, s32[2,32]{1,0:T(2,128)} %bitcast.14, s32[1,32]{1,0:T(1,128)} %chan_ref.1, s32[1,32]{1,0:T(1,128)} %count_ref.1, f32[32,2,512]{2,1,0:T(2,128)} %bitcast.12, bf16[32,2,512]{2,1,0:T(2,128)(2,1)} %bitcast.13, f32[32,32]{1,0:T(8,128)} %taper_ref.1), custom_call_target="tpu_custom_call" | custom-call | tf_op jit(solution)/shard_map/pallas_call | solution.py:417
  29.4 1.6 %convert.2 = f32[2,1,2,128,128]{4,3,2,1,0:T(8,128)} convert(bf16[2,1,2,128,128]{4,3,2,1,0:T(8,128)(2,1)} %bitcast.11) | non-fusion elementwise | flops 65536 | bytes 393216 | tf_op jit(solution)/shard_map/reshape | solution.py:458

commit v4 on v2

--- a/solution.py
+++ b/solution.py
@@ -76,7 +76,7 @@
     tile_l, chan_l = tile_ref[...].astype(F32), chan_ref[...].astype(F32)
     row_l, col_l = offs_ref[0:1, :].astype(F32), offs_ref[1:2, :].astype(F32)
     count_l = count_ref[...].astype(F32)
-    kind = lax.rem(iota((16, SUB), 0), 4)
+    kind = iota((16, SUB), 0) & 3
     meta = jnp.where(
         kind == 0, jnp.broadcast_to(row_l, (16, SUB)),
         jnp.where(kind == 1, 1.0, jnp.broadcast_to(chan_l, (16, SUB))),
@@ -117,7 +117,7 @@
         jnp.broadcast_to(col_s, (SUB, 128)).astype(BF16),
         preferred_element_type=F32,
     )
-    hot_x = jnp.broadcast_to(slot_s, (SUB, slots * 32)) == iota((SUB, slots * 32), 1) // 32
+    hot_x = jnp.broadcast_to(slot_s, (SUB, slots * 32)) == iota((SUB, slots * 32), 1) >> 5
     spread_meta = jnp.dot(
         meta.astype(BF16), jnp.where(hot_x, 1.0, 0.0).astype(BF16), preferred_element_type=F32
     )
@@ -160,7 +160,7 @@
                 eb[rows, 8 * n + 4 + kt, :] = val[1]
 
     sub8 = iota((8, 128), 0)
-    bit0, bit1, bit2 = lax.rem(sub8, 2) == 1, lax.rem(sub8 // 2, 2) == 1, sub8 >= 4
+    bit0, bit1, bit2 = (sub8 & 1) == 1, (sub8 & 2) == 2, sub8 >= 4
     taper = taper_ref[...]
     taper = jnp.concatenate([taper, taper], 1)
     taper = jnp.concatenate([taper, taper], 0)
@@ -223,7 +223,7 @@
     lax.fori_loop(0, SUB // group, sub_group, 0)
 
     def turns_of(rows, cols):
-        prod = (lax.rem(rows, 32) - 16) * (lax.rem(cols, 32) - 16)
+        prod = ((rows & 31) - 16) * ((cols & 31) - 16)
         return prod.astype(F32) * (-1.0 / 32.0)
 
     def quarter(n):
@@ -231,21 +231,21 @@
 
     rows, cols = iota((64, 128), 0), iota((64, 128), 1)
     right = unit_phase(
-        turns_of(rows, cols) + quarter(cols // 64 + rows // 32 - lax.rem(cols // 32, 2))
+        turns_of(rows, cols) + quarter((cols >> 6) + (rows >> 5) - ((cols >> 5) & 1))
     )[0]
     right_h = right.astype(BF16)
     right_l = (right - right_h.astype(F32)).astype(BF16)
     right = jnp.concatenate([right_h, right_l, right_h, jnp.zeros((64, 128), BF16)], 0)
     rows, cols = iota((64, 64), 0), iota((64, 64), 1)
-    left = unit_phase(turns_of(rows, cols) + quarter(cols // 32 - rows // 32))[0]
+    left = unit_phase(turns_of(rows, cols) + quarter((cols >> 5) - (rows >> 5)))[0]
     left = (left * (1.0 / 32.0)).astype(BF16)
     rows, cols = iota((128, 512), 0), iota((128, 512), 1)
     repeat = jnp.where(
-        (rows // 32 == cols // 128) & (lax.rem(rows, 32) == lax.rem(cols, 32)), 1.0, 0.0
+        ((rows >> 5) == (cols >> 7)) & ((rows & 31) == (cols & 31)), 1.0, 0.0
     ).astype(BF16)
 
     y_scr[...] = jnp.dot(g_scr[...], right, preferred_element_type=F32).astype(BF16)
-    lane32 = lax.rem(iota((32, 128), 1), 32)
+    lane32 = iota((32, 128), 1) & 31
     src_copy.wait()
 
     def second(s, carry):
@@ -259,29 +259,33 @@
         )
         return carry
 
-    lax.fori_loop(0, SUB, second, 0, unroll=16)
+    lax.fori_loop(0, SUB, second, 0, unroll=32)
 
     low_half = iota((32, 128), 1) < 64
-    for pair in range(slots // 2):
-        left_z = z_scr[jnp.clip(src_s[0, 2 * pair], 0, SUB - 1)]
-        right_z = pltpu.roll(z_scr[jnp.clip(src_s[0, 2 * pair + 1], 0, SUB - 1)], 64, 1)
-        d, j = pair // (cap // 2), pair % (cap // 2)
-        send[d, 32 * j:32 * j + 32, :] = jnp.where(low_half, left_z, right_z).astype(BF16)
+
+    def fill(d):
+        for j in range(cap // 2):
+            at = d * cap + 2 * j
+            left_z = z_scr[jnp.clip(src_s[0, at], 0, SUB - 1)]
+            right_z = pltpu.roll(z_scr[jnp.clip(src_s[0, at + 1], 0, SUB - 1)], 64, 1)
+            send[d, 32 * j:32 * j + 32, :] = jnp.where(low_half, left_z, right_z).astype(BF16)
 
     pl.semaphore_wait(barrier, n_span + n_freq - 2)
     moves = []
     for o in range(1, n_span):
         to = lax.rem(me_s + o, n_span)
+        fill(to)
         move = pltpu.make_async_remote_copy(
             src_ref=send.at[to], dst_ref=got.at[o - 1], send_sem=a_send.at[o - 1],
             recv_sem=a_recv.at[o - 1], device_id=(to, me_f), device_id_type=MESH,
         )
         move.start()
         moves.append(move)
+    fill(me_s)
 
     channels = CH_DEV * n_freq
     lane = iota((1, 128), 1)
-    lane_a = lax.rem(lane, 32).astype(F32)
+    lane_a = (lane & 31).astype(F32)
     cell_row = iota((TILE, 128), 0).astype(F32)
 
     def widen(block, n):

time: 28.6 us -> 28.5 us (level)
  no operation moved by 1% of the time
where the time goes in v4:
time: 28.5 us; the launch traced here: 28.4 us
  Pallas kernels  26.7 us (94%)
  other arithmetic  1.63 us (6%)
    pallas_call x1, Pallas kernels, body(): pl.pallas_call(functools.partial(kernel, n_span, n_freq, cap, rows_per),...  26.7 us
    reshape x1, other arithmetic, body(): return out[:, :2 * TILE].astype(F32).reshape(NT, 1, 2, TILE, TILE)  1.63 us

profile of v4, /device:TPU:0, one launch (start us, length us, event | category | flops | bytes accessed | tf_op | source)
XLA Modules:
  0.0 28.4 jit_solution(109690327628421851)
XLA Ops:
  0.0 26.7 %shard_map.73 = bf16[2,256,128]{2,1,0:T(8,128)(2,1)} custom-call(s32[1,32]{1,0:T(1,128)} %bitcast.15, s32[2,32]{1,0:T(2,128)} %bitcast.14, s32[1,32]{1,0:T(1,128)} %chan_ref.1, s32[1,32]{1,0:T(1,128)} %count_ref.1, f32[32,2,512]{2,1,0:T(2,128)} %bitcast.12, bf16[32,2,512]{2,1,0:T(2,128)(2,1)} %bitcast.13, f32[32,32]{1,0:T(8,128)} %taper_ref.1), custom_call_target="tpu_custom_call" | custom-call | tf_op jit(solution)/shard_map/pallas_call | solution.py:409
  26.8 1.6 %convert.2 = f32[2,1,2,128,128]{4,3,2,1,0:T(8,128)} convert(bf16[2,1,2,128,128]{4,3,2,1,0:T(8,128)(2,1)} %bitcast.11) | non-fusion elementwise | flops 65536 | bytes 393216 | tf_op jit(solution)/shard_map/reshape | solution.py:448

commit v5 on v1

--- a/solution.py
+++ b/solution.py
@@ -44,7 +44,7 @@
 def kernel(
     n_span, n_freq, cap, rows_per, tile_ref, offs_ref, chan_ref, count_ref, coord_ref, vis_ref,
     taper_ref, out_ref, ea, eb, g_scr, y_scr, z_scr, rhs_scr, src_v, src_s, send, got, acc_scr,
-    rs_send, rs_got, ag_send, ag_got, src_sem, a_send, a_recv, r_send, r_recv, g_send, g_recv,
+    rs_send, rs_got, src_sem, a_send, a_recv, r_send, r_recv, g_send, g_recv,
 ):
     me_s, me_f = lax.axis_index("span"), lax.axis_index("freq")
     barrier = pltpu.get_barrier_semaphore()
@@ -65,7 +65,7 @@
     tile_l, chan_l = tile_ref[...].astype(F32), chan_ref[...].astype(F32)
     row_l, col_l = offs_ref[0:1, :].astype(F32), offs_ref[1:2, :].astype(F32)
     count_l = count_ref[...].astype(F32)
-    kind = lax.rem(iota((16, SUB), 0), 4)
+    kind = iota((16, SUB), 0) & 3
     meta = jnp.where(
         kind == 0, jnp.broadcast_to(row_l, (16, SUB)),
         jnp.where(kind == 1, 1.0, jnp.broadcast_to(chan_l, (16, SUB))),
@@ -106,7 +106,7 @@
         jnp.broadcast_to(col_s, (SUB, 128)).astype(BF16),
         preferred_element_type=F32,
     )
-    hot_x = jnp.broadcast_to(slot_s, (SUB, slots * 32)) == iota((SUB, slots * 32), 1) // 32
+    hot_x = jnp.broadcast_to(slot_s, (SUB, slots * 32)) == iota((SUB, slots * 32), 1) >> 5
     spread_meta = jnp.dot(
         meta.astype(BF16), jnp.where(hot_x, 1.0, 0.0).astype(BF16), preferred_element_type=F32
     )
@@ -149,7 +149,7 @@
         eb[2 * n + 1] = val[1]
 
     sub8 = iota((8, kk), 0)
-    bit0, bit1, bit2 = lax.rem(sub8, 2) == 1, lax.rem(sub8 // 2, 2) == 1, sub8 >= 4
+    bit0, bit1, bit2 = (sub8 & 1) == 1, (sub8 & 2) == 2, sub8 >= 4
     taper = taper_ref[...]
     taper = jnp.concatenate([taper, taper], 1)
     taper = jnp.concatenate([taper, taper], 0)
@@ -196,7 +196,7 @@
     lax.fori_loop(0, SUB, one_sub, 0, unroll=4)
 
     def turns_of(rows, cols):
-        prod = (lax.rem(rows, 32) - 16) * (lax.rem(cols, 32) - 16)
+        prod = ((rows & 31) - 16) * ((cols & 31) - 16)
         return prod.astype(F32) * (-1.0 / 32.0)
 
     def quarter(n):
@@ -204,21 +204,21 @@
 
     rows, cols = iota((64, 128), 0), iota((64, 128), 1)
     right = unit_phase(
-        turns_of(rows, cols) + quarter(cols // 64 + rows // 32 - lax.rem(cols // 32, 2))
+        turns_of(rows, cols) + quarter((cols >> 6) + (rows >> 5) - ((cols >> 5) & 1))
     )[0]
     right_h = right.astype(BF16)
     right_l = (right - right_h.astype(F32)).astype(BF16)
     right = jnp.concatenate([right_h, right_l, right_h, jnp.zeros((64, 128), BF16)], 0)
     rows, cols = iota((64, 64), 0), iota((64, 64), 1)
-    left = unit_phase(turns_of(rows, cols) + quarter(cols // 32 - rows // 32))[0]
+    left = unit_phase(turns_of(rows, cols) + quarter((cols >> 5) - (rows >> 5)))[0]
     left = (left * (1.0 / 32.0)).astype(BF16)
     rows, cols = iota((128, 512), 0), iota((128, 512), 1)
     repeat = jnp.where(
-        (rows // 32 == cols // 128) & (lax.rem(rows, 32) == lax.rem(cols, 32)), 1.0, 0.0
+        ((rows >> 5) == (cols >> 7)) & ((rows & 31) == (cols & 31)), 1.0, 0.0
     ).astype(BF16)
 
     y_scr[...] = jnp.dot(g_scr[...], right, preferred_element_type=F32).astype(BF16)
-    lane32 = lax.rem(iota((32, 128), 1), 32)
+    lane32 = iota((32, 128), 1) & 31
     src_copy.wait()
 
     def second(s, carry):
@@ -232,39 +232,44 @@
         )
         return carry
 
-    lax.fori_loop(0, SUB, second, 0, unroll=8)
+    lax.fori_loop(0, SUB, second, 0, unroll=32)
 
     low_half = iota((32, 128), 1) < 64
-    for pair in range(slots // 2):
-        left_z = z_scr[jnp.clip(src_s[0, 2 * pair], 0, SUB - 1)]
-        right_z = pltpu.roll(z_scr[jnp.clip(src_s[0, 2 * pair + 1], 0, SUB - 1)], 64, 1)
-        d, j = pair // (cap // 2), pair % (cap // 2)
-        send[d, 32 * j:32 * j + 32, :] = jnp.where(low_half, left_z, right_z).astype(BF16)
+
+    def fill(d):
+        for j in range(cap // 2):
+            at = d * cap + 2 * j
+            left_z = z_scr[jnp.clip(src_s[0, at], 0, SUB - 1)]
+            right_z = pltpu.roll(z_scr[jnp.clip(src_s[0, at + 1], 0, SUB - 1)], 64, 1)
+            send[d, 32 * j:32 * j + 32, :] = jnp.where(low_half, left_z, right_z).astype(BF16)
 
     pl.semaphore_wait(barrier, n_span + n_freq - 2)
     moves = []
     for o in range(1, n_span):
         to = lax.rem(me_s + o, n_span)
+        fill(to)
         move = pltpu.make_async_remote_copy(
             src_ref=send.at[to], dst_ref=got.at[o - 1], send_sem=a_send.at[o - 1],
             recv_sem=a_recv.at[o - 1], device_id=(to, me_f), device_id_type=MESH,
         )
         move.start()
         moves.append(move)
+    fill(me_s)
 
     channels = CH_DEV * n_freq
     lane = iota((1, 128), 1)
-    lane_a = lax.rem(lane, 32).astype(F32)
+    lane_a = (lane & 31).astype(F32)
     cell_row = iota((TILE, 128), 0).astype(F32)
-    cell_col = iota((32, 128), 1).astype(F32)
+    cell_col = iota((8, 128), 1).astype(F32)
 
     def widen(block, n):
         wide = jnp.dot(block[0:data_rows, :], repeat, preferred_element_type=F32)
         info = block[data_rows:, :].astype(F32)
         for i in range(cap):
             j, h = i // 2, i % 2
-            off = cell_col - jnp.broadcast_to(info[i:i + 1, :], (32, 128))
-            inside = (off >= 0.0) & (off < 32.0)
+            off = cell_col - jnp.broadcast_to(info[i:i + 1, :], (8, 128))
+            inside = jnp.where((off >= 0.0) & (off < 32.0), 1.0, 0.0)
+            inside = jnp.concatenate([inside] * 4, 0) > 0.5
             part = wide[32 * j:32 * j + 32, 256 * h:256 * h + 256]
             rhs_scr[n, 32 * i:32 * i + 32, 0:128] = jnp.where(
                 inside, part[:, :128], 0.0
@@ -342,24 +347,22 @@
         for o in range(1, n_freq):
             sums[term][o - 1].wait_recv()
             total = total + rs_got[term, o - 1].astype(F32)
-        ag_send[term] = (total * scale).astype(BF16)
+        mine = out_ref.at[term, peer_rows(me_f)]
+        mine[...] = (total * scale).astype(BF16)
         started = []
         for o in range(1, n_freq):
             to = lax.rem(me_f + o, n_freq)
             move = pltpu.make_async_remote_copy(
-                src_ref=ag_send.at[term], dst_ref=ag_got.at[term, o - 1],
+                src_ref=mine, dst_ref=mine,
                 send_sem=g_send.at[term, o - 1], recv_sem=g_recv.at[term, o - 1],
                 device_id=(me_s, to), device_id_type=MESH,
             )
             move.start()
             started.append(move)
         gathers.append(started)
-        out_ref[term, peer_rows(me_f), :] = ag_send[term].astype(F32)
     for term in range(NT):
         for o in range(1, n_freq):
             gathers[term][o - 1].wait_recv()
-            frm = lax.rem(me_f - o + n_freq, n_freq)
-            out_ref[term, peer_rows(frm), :] = ag_got[term, o - 1].astype(F32)
     for move in moves + sums[0] + sums[1] + gathers[0] + gathers[1]:
         move.wait_send()
 
@@ -375,7 +378,7 @@
     block = cap * 16 + 16
     out = pl.pallas_call(
         functools.partial(kernel, n_span, n_freq, cap, rows_per),
-        out_shape=jax.ShapeDtypeStruct((NT, n_freq * rows_per, 128), F32),
+        out_shape=jax.ShapeDtypeStruct((NT, n_freq * rows_per, 128), BF16),
         in_specs=[pl.BlockSpec(memory_space=pltpu.VMEM)] * 7,
         out_specs=pl.BlockSpec(memory_space=pltpu.VMEM),
         scratch_shapes=[
@@ -392,8 +395,6 @@
             pltpu.VMEM((NT, n_freq * rows_per, 128), F32),
             pltpu.VMEM((NT, n_freq * rows_per, 128), BF16),
             pltpu.VMEM((NT, n_freq - 1, rows_per, 128), BF16),
-            pltpu.VMEM((NT, rows_per, 128), BF16),
-            pltpu.VMEM((NT, n_freq - 1, rows_per, 128), BF16),
             dma(()),
             dma((n_span - 1,)), dma((n_span - 1,)),
             dma((NT, n_freq - 1)), dma((NT, n_freq - 1)),
@@ -405,7 +406,7 @@
     )(
         cover_tile[:, :, 0], offsets[0].T, channel, vis_counts, coords[0], visibilities[0], taper,
     )
-    return out[:, :2 * TILE].reshape(NT, 1, 2, TILE, TILE)
+    return out[:, :2 * TILE].astype(F32).reshape(NT, 1, 2, TILE, TILE)
 
 
 def solution(mesh):

time: 28.4 us -> 27.7 us (0.975)
  other arithmetic: 0 us -> 0.72 us
  local copies, waits for them, and re-layouts: 3.87 us -> 3.17 us
  Pallas kernels: 24.3 us -> 23.6 us
    reshape x0 -> x1, other arithmetic: none -> 0.72 us  [body(): return out[:, :2 * TILE].astype(F32).reshape(NT, 1, 2, TILE, TILE)]
    unnamed x15 -> x14, local copies, waits for them, and re-layouts: 3.87 us -> 3.17 us
    pallas_call x1, Pallas kernels: 24.3 us -> 23.6 us  [body(): pl.pallas_call(functools.partial(kernel, n_span, n_freq, cap, rows_per),...]
where the time goes in v5:
time: 27.7 us; the launch traced here: 27.5 us
  Pallas kernels  23.6 us (85%)
  local copies, waits for them, and re-layouts  3.17 us (11%)
  other arithmetic  0.72 us (3%)
    pallas_call x1, Pallas kernels, body(): pl.pallas_call(functools.partial(kernel, n_span, n_freq, cap, rows_per),...  23.6 us
    unnamed x14, local copies, waits for them, and re-layouts  3.17 us
    reshape x1, other arithmetic, body(): return out[:, :2 * TILE].astype(F32).reshape(NT, 1, 2, TILE, TILE)  0.72 us

profile of v5, /device:TPU:0, one launch (start us, length us, event | category | flops | bytes accessed | tf_op | source)
XLA Modules:
  0.0 27.5 jit_solution(7267701019230636589)
XLA Ops:
  0.0 0.0 copy-start.5
  0.0 0.0 copy-start.6
  0.0 0.0 copy-start.3
  0.0 0.0 copy-start.4
  0.0 0.6 %copy-done.5 = s32[1,32]{1,0:T(1,128)S(1)} copy-done((s32[1,32]{1,0:T(1,128)S(1)}, s32[1,32]{1,0:T(1,128)}, u32[]{:S(2)}) %copy-start.5) | copy-done | bytes 152
  0.7 0.0 copy-done.6
  0.7 0.0 copy-done.3
  0.7 0.0 copy-done.4
  0.7 0.0 copy-start
  0.7 0.9 %copy-done = f32[1,32,2,512]{3,2,1,0:T(2,128)S(1)} copy-done((f32[1,32,2,512]{3,2,1,0:T(2,128)S(1)}, f32[1,32,2,512]{3,2,1,0:T(2,128)}, u32[]{:S(2)}) %copy-start) | copy-done | bytes 131096
  1.6 0.0 copy-start.1
  1.6 0.8 %copy-done.1 = bf16[1,32,2,512]{3,2,1,0:T(2,128)(2,1)S(1)} copy-done((bf16[1,32,2,512]{3,2,1,0:T(2,128)(2,1)S(1)}, bf16[1,32,2,512]{3,2,1,0:T(2,128)(2,1)}, u32[]{:S(2)}) %copy-start.1) | copy-done | bytes 65560
  2.5 0.0 copy-start.2
  2.5 0.7 %copy-done.2 = f32[32,32]{1,0:T(8,128)S(1)} copy-done((f32[32,32]{1,0:T(8,128)S(1)}, f32[32,32]{1,0:T(8,128)}, u32[]{:S(2)}) %copy-start.2) | copy-done | bytes 4120
  3.2 23.6 %shard_map.73 = bf16[2,256,128]{2,1,0:T(8,128)(2,1)S(1)} custom-call(s32[1,32]{1,0:T(1,128)S(1)} %bitcast.15, s32[2,32]{1,0:T(2,128)S(1)} %bitcast.14, s32[1,32]{1,0:T(1,128)S(1)} %copy-done.5, s32[1,32]{1,0:T(1,128)S(1)} %copy-done.6, f32[32,2,512]{2,1,0:T(2,128)S(1)} %bitcast.12, bf16[32,2,512]{2,1,0:T(2,128)(2,1)S(1)} %bitcast.13, f32[32,32]{1,0:T(8,128)S(1)} %copy-done.2), custom_call_target="tpu_custom_call" | custom-call | tf_op jit(solution)/shard_map/pallas_call | solution.py:379
  26.8 0.7 %convert.2 = f32[2,1,2,128,128]{4,3,2,1,0:T(8,128)} convert(bf16[2,1,2,128,128]{4,3,2,1,0:T(8,128)(2,1)S(1)} %bitcast.11) | non-fusion elementwise | flops 65536 | bytes 393216 | tf_op jit(solution)/shard_map/reshape | solution.py:409
Async XLA Ops:
  0.0 0.7 %copy-start.5 = (s32[1,32]{1,0:T(1,128)S(1)}, s32[1,32]{1,0:T(1,128)}, u32[]{:S(2)}) copy-start(s32[1,32]{1,0:T(1,128)} %chan_ref.1) | copy-start | bytes 388
  0.0 0.7 %copy-start.6 = (s32[1,32]{1,0:T(1,128)S(1)}, s32[1,32]{1,0:T(1,128)}, u32[]{:S(2)}) copy-start(s32[1,32]{1,0:T(1,128)} %count_ref.1) | copy-start | bytes 388
  0.0 0.7 %copy-start.3 = (s32[1,32,2]{1,2,0:T(2,128)S(1)}, s32[1,32,2]{1,2,0:T(2,128)}, u32[]{:S(2)}) copy-start(s32[1,32,2]{1,2,0:T(2,128)} %param.11) | copy-start | bytes 772
  0.0 0.7 %copy-start.4 = (s32[1,32,1]{1,2,0:T(1,128)S(1)}, s32[1,32,1]{1,2,0:T(1,128)}, u32[]{:S(2)}) copy-start(s32[1,32,1]{1,2,0:T(1,128)} %param.10) | copy-start | bytes 388
  0.7 0.9 %copy-start = (f32[1,32,2,512]{3,2,1,0:T(2,128)S(1)}, f32[1,32,2,512]{3,2,1,0:T(2,128)}, u32[]{:S(2)}) copy-start(f32[1,32,2,512]{3,2,1,0:T(2,128)} %param.8) | copy-start | bytes 393220
  1.6 0.8 %copy-start.1 = (bf16[1,32,2,512]{3,2,1,0:T(2,128)(2,1)S(1)}, bf16[1,32,2,512]{3,2,1,0:T(2,128)(2,1)}, u32[]{:S(2)}) copy-start(bf16[1,32,2,512]{3,2,1,0:T(2,128)(2,1)} %param.7) | copy-start | bytes 196612
  2.5 0.7 %copy-start.2 = (f32[32,32]{1,0:T(8,128)S(1)}, f32[32,32]{1,0:T(8,128)}, u32[]{:S(2)}) copy-start(f32[32,32]{1,0:T(8,128)} %taper_ref.1) | copy-start | bytes 12292
